TPU v7x, 32 devices: a whole 2x2x4 slice. The times are simulated.
32 devices in a mesh: layer: 4 (over y, core), feat: 8 (over z, x).
Axes of the slice: x: 2, y: 2, z: 4, core: 2. Of those that a mesh axis runs over, the one named last changes fastest.
Arguments:
- resid_stream: bfloat16 [8, 4, 2304], P('feat', 'layer'), may hold values from -6 to 6
- enc_mantissa: bfloat16 [4, 2304, 16384], P('layer', None, 'feat'), may hold values from -96 to 96
- enc_exponent: int32 [4, 18, 128], P('layer', None, 'feat'), may hold values from -11 to -10
- enc_bias: float32 [4, 16384], P('layer', 'feat'), may hold values from -3 to 3
- dec_weight: bfloat16 [10, 16384, 2304], P(None, 'feat', 'layer'), may hold values from -0.046875 to 0.046875
- dec_bias: float32 [4, 2304], P('layer'), may hold values from -3 to 3
Outputs:
- recon: bfloat16 [8, 4, 2304], P('feat', 'layer')
All inputs are finite; a program needn't handle non-finite values.
Results may differ from a plain program's by a relative error of at most 0.0044.
Values may be sent and summed in bfloat16 or wider, within the bound.
No kernel may reach another device: no remote copies, remote signals or barrier semaphores. Data moves between devices by JAX's collectives and lax.ppermute only.
A program may use at most 128 MiB of HBM per device.

v0:
```python
import jax
import jax.numpy as jnp
from jax import lax
from jax.sharding import PartitionSpec as P

BLK = 128


def shards(resid_stream, enc_mantissa, enc_exponent, enc_bias, dec_weight, dec_bias):
    layer_count = lax.axis_size("layer")
    width = resid_stream.shape[2]
    feat_local = enc_mantissa.shape[2]
    col_local = dec_weight.shape[2]
    tok_local = resid_stream.shape[0]
    scales = jnp.exp2(enc_exponent[0].astype(jnp.float32))
    blocks = enc_mantissa[0].astype(jnp.float32).reshape(width // BLK, BLK, feat_local // BLK, BLK)
    weight = (blocks * scales[:, None, :, None]).reshape(width, feat_local).astype(jnp.bfloat16)
    bias_row = enc_bias[0][None, :]
    pre_act = jnp.dot(
        lax.all_gather(resid_stream, "feat", axis=0, tiled=True)[:, 0, :],
        weight,
        preferred_element_type=jnp.float32,
    )
    latent = jnp.maximum(pre_act + bias_row, 0.0).astype(jnp.bfloat16)
    stacked = lax.all_gather(latent[None], "layer", axis=0, tiled=True)
    columns = []
    for target in range(layer_count):
        total = jnp.zeros((tok_local * lax.axis_size("feat"), col_local), jnp.float32)
        for source in range(target + 1):
            pair_index = target * (target + 1) // 2 + source
            total = total + jnp.dot(
                stacked[source], dec_weight[pair_index], preferred_element_type=jnp.float32
            )
        columns.append(total)
    summed = lax.psum_scatter(jnp.stack(columns, axis=1), "feat", scatter_dimension=0, tiled=True)
    finished = lax.all_to_all(summed, "layer", split_axis=1, concat_axis=2, tiled=True)
    return (finished + dec_bias[0][None, None, :]).astype(jnp.bfloat16)


def solution(mesh):
    in_specs = (
        P("feat", "layer", None),
        P("layer", None, "feat"),
        P("layer", None, "feat"),
        P("layer", "feat"),
        P(None, "feat", "layer"),
        P("layer", None),
    )
    out_specs = P("feat", "layer", None)
    return jax.shard_map(shards, mesh=mesh, in_specs=in_specs, out_specs=out_specs, check_vma=False)
```

profile of v0, /device:TPU:0, one launch (start us, length us, event | category | flops | bytes accessed | tf_op | source)
XLA Modules:
  0.0 181.2 jit_solution(3151799212801999939)
XLA Ops:
  6.5 0.0 all-reduce.3.cloned.1.call-start
  6.5 12.6 %convert_bitcast_fusion = f32[288,8,16,128]{3,1,2,0:T(8,128)} fusion(bf16[1,2304,2048]{2,1,0:T(8,128)(2,1)} %param.7), kind=kLoop, calls=%fused_computation.2 | loop fusion | flops 4718592 | bytes 28311552
  19.1 0.0 copy-start.2
  19.1 0.0 copy-start.1
  19.1 18.0 %copy.16 = f32[288,8,16,128]{3,2,1,0:T(8,128)} copy(f32[288,8,16,128]{3,1,2,0:T(8,128)} %convert_bitcast_fusion) | data formatting | bytes 37748736
  37.1 0.0 copy-done.2
  37.1 0.1 copy.12
  37.2 0.0 copy-done.1
  37.2 32.3 %all_gather.6 = bf16[8,1,2304]{2,1,0:T(2,128)(2,1)S(1)} all-gather(bf16[1,1,2304]{2,1,0:T(2,128)(2,1)S(1)} %copy-done.1), channel_id=1, replica_groups=mesh['layer'=4,'feat'=8] {'feat'}, dimensions={0}, use_global_device_ids=true | all-gather | bytes 41472 | tf_op jit(solution)/shard_map/all_gather | solution.py:20
  69.6 0.0 copy-start.3
  69.6 0.0 slice-start
  69.6 0.0 slice-start.1
  69.6 0.0 slice-start.2
  69.6 0.0 slice-start.3
  69.6 9.8 %fusion = bf16[18,128,16,128]{3,2,1,0:T(8,128)(2,1)S(1)} fusion(f32[18,16]{1,0:T(8,128)S(1)} %copy.12, f32[18,128,16,128]{3,2,1,0:T(8,128)} %bitcast.93), kind=kLoop, calls=%fused_computation.1 | loop fusion | flops 9437184 | bytes 28312704 | tf_op jit(solution)/shard_map/convert_element_type | solution.py:17
  79.4 0.0 copy-done.3
  79.4 0.0 slice-start.4
  79.4 0.0 slice-start.5
  79.4 1.3 fusion.43
  80.8 5.5 %all-gather = bf16[32,2048]{1,0:T(8,128)(2,1)S(1)} all-gather(bf16[8,2048]{1,0:T(8,128)(2,1)S(1)} %fusion.43), channel_id=2, replica_groups=mesh['layer'=4,'feat'=8] {'layer'}, dimensions={0}, use_global_device_ids=true | all-gather | bytes 163840 | tf_op jit(solution)/shard_map/all_gather | solution.py:25
  86.3 2.4 %fusion.4 = f32[8,576]{1,0:T(8,128)S(1)} fusion(bf16[10,2048,576]{1,2,0:T(8,128)(2,1)} %param.10, bf16[32,2048]{1,0:T(8,128)(2,1)S(1)} %all-gather), kind=kOutput, calls=%fused_computation.6 | convolution fusion | flops 18874368 | bytes 2410496 | tf_op jit(solution)/shard_map/dot_general | solution.py:31
  88.7 0.0 slice-done
  88.7 0.0 slice-done.1
  88.7 0.0 slice-done.2
  88.7 0.0 slice-done.3
  88.7 0.0 slice-done.4
  88.7 0.0 slice-done.5
  88.8 0.7 fusion.6
  89.5 0.0 copy-start.4
  89.5 0.0 copy-start
  89.5 0.7 fusion.8
  90.2 0.7 fusion.12
  90.9 0.7 fusion.14
  91.6 0.7 fusion.18
  92.4 0.7 fusion.46
  93.1 0.7 fusion.52
  93.8 0.7 fusion.61
  94.5 0.7 fusion.73
  95.3 0.7 copy.13
  95.9 0.0 all-reduce.3.cloned.1.call-update
  96.0 0.0 copy-done.4
  96.0 0.6 dynamic-slice
  96.6 69.3 %all-reduce.3.cloned.1.call-done = f32[8,4,576]{2,1,0:T(4,128)} async-done(((f32[8,4,576]{2,1,0:T(4,128)}), f32[8,4,576]{2,1,0:T(4,128)}) %all-reduce.3.cloned.1.call-update) | async-done | bytes 73744
  165.8 1.3 constant_dynamic-slice_fusion
  167.2 6.4 %all_to_all.12 = f32[1,4,576]{2,0,1:T(1,128)S(1)} all-to-all(f32[1,4,576]{2,0,1:T(1,128)S(1)} %copy.14), channel_id=1, replica_groups=mesh['layer'=4,'feat'=8] {'layer'}, dimensions={1} | all-to-all | bytes 18432 | tf_op jit(solution)/shard_map/all_to_all | solution.py:36
  173.6 0.1 all_to_all.10
  173.7 0.0 copy-done
  173.7 0.6 fusion.88
  (5 shorter events, 0.1 us)
Async XLA Ops:
  6.5 159.3 %all-reduce.3.cloned.1.call-start = ((), (), s32[]{:S(2)}) async-start(), calls=%async_computation.1 | async-start | bytes 163840
  19.1 18.0 %copy-start.2 = (s32[1,18,16]{1,2,0:T(8,128)S(1)}, s32[1,18,16]{1,2,0:T(8,128)}, u32[]{:S(2)}) copy-start(s32[1,18,16]{1,2,0:T(8,128)} %param.8) | copy-start | bytes 3460
  19.1 18.1 %copy-start.1 = (bf16[1,1,2304]{2,1,0:T(2,128)(2,1)S(1)}, bf16[1,1,2304]{2,1,0:T(2,128)(2,1)}, u32[]{:S(2)}) copy-start(bf16[1,1,2304]{2,1,0:T(2,128)(2,1)} %param.6) | copy-start | bytes 13828
  69.6 9.8 %copy-start.3 = (f32[1,2048]{1,0:T(1,128)S(1)}, f32[1,2048]{1,0:T(1,128)}, u32[]{:S(2)}) copy-start(f32[1,2048]{1,0:T(1,128)} %param.9) | copy-start | bytes 24580
  69.6 19.1 %slice-start = ((s8[23592960]{0:T(1024)(128)(4,1)}), s8[4194304]{0:T(1024)(128)(4,1)S(1)}, s32[]{:S(2)}) async-start(s8[23592960]{0:T(1024)(128)(4,1)} %bitcast.94), calls=%async_computation.2 | async-start | bytes 8388608
  69.6 19.1 %slice-start.1 = ((s8[23592960]{0:T(1024)(128)(4,1)}), s8[4194304]{0:T(1024)(128)(4,1)S(1)}, s32[]{:S(2)}) async-start(s8[23592960]{0:T(1024)(128)(4,1)} %bitcast.94), calls=%async_computation.3 | async-start | bytes 8388608
  69.6 19.1 %slice-start.2 = ((s8[23592960]{0:T(1024)(128)(4,1)}), s8[4194304]{0:T(1024)(128)(4,1)S(1)}, s32[]{:S(2)}) async-start(s8[23592960]{0:T(1024)(128)(4,1)} %bitcast.94), calls=%async_computation.4 | async-start | bytes 8388608
  69.6 19.1 %slice-start.3 = ((s8[23592960]{0:T(1024)(128)(4,1)}), s8[4194304]{0:T(1024)(128)(4,1)S(1)}, s32[]{:S(2)}) async-start(s8[23592960]{0:T(1024)(128)(4,1)} %bitcast.94), calls=%async_computation.5 | async-start | bytes 8388608
  79.4 9.3 %slice-start.4 = ((s8[23592960]{0:T(1024)(128)(4,1)}), s8[4194304]{0:T(1024)(128)(4,1)S(1)}, s32[]{:S(2)}) async-start(s8[23592960]{0:T(1024)(128)(4,1)} %bitcast.94), calls=%async_computation.6 | async-start | bytes 8388608
  79.4 9.3 %slice-start.5 = ((s8[23592960]{0:T(1024)(128)(4,1)}), s8[2621440]{0:T(1024)(128)(4,1)S(1)}, s32[]{:S(2)}) async-start(s8[23592960]{0:T(1024)(128)(4,1)} %bitcast.94), calls=%async_computation.7 | async-start | bytes 5242880
  89.5 6.5 %copy-start.4 = (u32[32]{0:T(128)S(1)}, u32[32]{0:T(128)}, u32[]{:S(2)}) copy-start(u32[32]{0:T(128)} %constant.11) | copy-start | bytes 388
  89.5 84.3 %copy-start = (f32[1,2304]{1,0:T(1,128)S(1)}, f32[1,2304]{1,0:T(1,128)}, u32[]{:S(2)}) copy-start(f32[1,2304]{1,0:T(1,128)} %param.11) | copy-start | bytes 27652
Sparse Core Ops, SparseCore 0:
  96.1 69.7 all-reduce.2
where the time goes:
time: 182 us; the launch traced here: 181 us
  waiting for transfers between devices  69.3 us (38%)
  blocking collectives  44.2 us (24%)
  other arithmetic  23 us (13%)
  local copies, waits for them, and re-layouts  20.9 us (11%)
  between operations  13.5 us (7%)
  matrix products  10.2 us (6%)
    unnamed x2, waiting for transfers between devices  69.3 us
    all_gather x1, blocking collectives, shards(): lax.all_gather(resid_stream, 'feat', axis=0, tiled=True)[:, 0, :]  32.3 us
    unnamed x25, local copies, waits for them, and re-layouts  20 us
    unnamed x2, other arithmetic  12.6 us
    convert_element_type x1, other arithmetic, shards(): (blocks * scales[:, None, :, None]).reshape(width, feat_local)  9.81 us
    dot_general x10, matrix products, shards(): jnp.dot(stacked[source], dec_weight[pair_index], preferred_element_type=j...  8.87 us
    all_to_all x1, blocking collectives, shards(): lax.all_to_all(summed, 'layer', split_axis=1, concat_axis=2, tiled=True)  6.37 us
    all_gather x1, blocking collectives, shards(): stacked = lax.all_gather(latent[None], 'layer', axis=0, tiled=True)  5.54 us
  transfers between devices with their start and end apart: 1, of which 1 were waited for; matrix products, arithmetic and copies ran while one was open for 0% of the time, Pallas kernels for 0%

commit v1 on v0

v1 whole, which is shorter than its diff:
```python
import jax
import jax.numpy as jnp
from jax import lax
from jax.experimental import pallas as pl
from jax.experimental.pallas import tpu as pltpu
from jax.sharding import PartitionSpec as P

BLK = 128
VMEM = pl.BlockSpec(memory_space=pltpu.VMEM)
LIMIT = 12 * 1024 * 1024


def encode_kernel(x_ref, mantissa_ref, exponent_ref, bias_ref, latent_ref):
    x = x_ref[...].astype(jnp.float32)
    tokens, width = x.shape
    features = mantissa_ref.shape[1]
    rows, blocks = exponent_ref.shape
    scale = jnp.exp2(exponent_ref[...].astype(jnp.float32)).astype(jnp.bfloat16)
    row_of = lax.broadcasted_iota(jnp.int32, (rows, width), 1) // BLK
    spread = (row_of == lax.broadcasted_iota(jnp.int32, (rows, width), 0)).astype(jnp.bfloat16)
    scales = lax.dot_general(scale, spread, (((0,), (0,)), ((), ())), preferred_element_type=jnp.float32)
    for first in range(0, blocks, 2):
        group = range(first, min(first + 2, blocks))
        scaled = jnp.concatenate([x * scales[j : j + 1, :] for j in group], axis=0).astype(jnp.bfloat16)
        columns = slice(first * BLK, (first + len(group)) * BLK)
        product = jnp.dot(scaled, mantissa_ref[:, columns], preferred_element_type=jnp.float32)
        for at, j in enumerate(group):
            own = product[at * tokens : (at + 1) * tokens, at * BLK : (at + 1) * BLK]
            there = slice(j * BLK, (j + 1) * BLK)
            latent_ref[:, there] = jnp.maximum(own + bias_ref[:, there], 0.0).astype(latent_ref.dtype)


def decode_kernel(latent_ref, weight_ref, out_ref):
    layers, tokens, _ = latent_ref.shape
    for target in range(layers):
        total = None
        for source in range(target + 1):
            pair = target * (target + 1) // 2 + source
            part = lax.dot_general(
                latent_ref[source],
                weight_ref[pair],
                (((1,), (1,)), ((), ())),
                preferred_element_type=jnp.float32,
            )
            total = part if total is None else total + part
        for token in range(tokens):
            out_ref[target * tokens + token] = total[token : token + 1, :]


def finish_kernel(parts_ref, bias_ref, out_ref):
    layers, shards, columns = parts_ref.shape[0], parts_ref.shape[1], parts_ref.shape[3]
    for block in range(layers):
        there = slice(block * columns, (block + 1) * columns)
        total = parts_ref[block, 0]
        for shard in range(1, shards):
            total = total + parts_ref[block, shard]
        out_ref[:, 0, there] = (total + bias_ref[:, there]).astype(out_ref.dtype)


def shards(resid_stream, enc_mantissa, enc_exponent, enc_bias, dec_weight, dec_bias):
    layer_count, feat_count = lax.axis_size("layer"), lax.axis_size("feat")
    tok_local, _, width = resid_stream.shape
    tokens = tok_local * feat_count
    feat_local = enc_mantissa.shape[2]
    col_local = dec_weight.shape[2]
    params = pltpu.CompilerParams(vmem_limit_bytes=LIMIT)

    spread = jnp.broadcast_to(resid_stream, (feat_count, tok_local, 1, width)).reshape(tokens, 1, width)
    x = lax.all_to_all(spread, "feat", 0, 0, tiled=True).reshape(tokens, width)
    latent = pl.pallas_call(
        encode_kernel,
        out_shape=jax.ShapeDtypeStruct((tokens, feat_local), jnp.bfloat16),
        in_specs=[VMEM] * 4,
        out_specs=VMEM,
        compiler_params=params,
        name="encode",
    )(x, enc_mantissa[0], enc_exponent[0], enc_bias)
    stacked = lax.all_gather(latent[None], "layer", axis=0, tiled=True)
    parts = pl.pallas_call(
        decode_kernel,
        out_shape=jax.ShapeDtypeStruct((layer_count * tokens, 1, col_local), jnp.float32),
        in_specs=[VMEM] * 2,
        out_specs=VMEM,
        compiler_params=params,
        name="decode",
    )(stacked, jnp.swapaxes(dec_weight, 1, 2))
    arrived = lax.all_to_all(parts, ("layer", "feat"), 0, 0, tiled=True)
    return pl.pallas_call(
        finish_kernel,
        out_shape=jax.ShapeDtypeStruct((tok_local, 1, width), jnp.bfloat16),
        in_specs=[VMEM] * 2,
        out_specs=VMEM,
        compiler_params=params,
        name="finish",
    )(arrived.reshape(layer_count, feat_count, tok_local, col_local), dec_bias)


def solution(mesh):
    in_specs = (
        P("feat", "layer", None),
        P("layer", None, "feat"),
        P("layer", None, "feat"),
        P("layer", "feat"),
        P(None, "feat", "layer"),
        P("layer", None),
    )
    out_specs = P("feat", "layer", None)
    return jax.shard_map(shards, mesh=mesh, in_specs=in_specs, out_specs=out_specs, check_vma=False)
```

time: 182 us -> 52.5 us (0.29)
  waiting for transfers between devices: 69.3 us -> 5.93 us
  blocking collectives: 44.2 us -> 14.7 us
  other arithmetic: 23 us -> 1.59 us
  between operations: 13.5 us -> 0.03 us
  matrix products: 10.2 us -> 0 us
  Pallas kernels: 0 us -> 8.43 us
  starting transfers between devices: 0.01 us -> 7.25 us
  local copies, waits for them, and re-layouts: 20.9 us -> 14.1 us
    unnamed x2 -> x0, waiting for transfers between devices: 69.3 us -> none
    all_gather x1 -> x0, blocking collectives: 32.3 us -> none  [shards(): lax.all_gather(resid_stream, 'feat', axis=0, tiled=True)[:, 0, :]]
    unnamed x2 -> x1, other arithmetic: 12.6 us -> 0.75 us
    convert_element_type x2 -> x0, other arithmetic: 10.4 us -> none  [the longest x1 9.81 us: shards(): (blocks * scales[:, None, :, None]).reshape(width, feat_local)]
    dot_general x11 -> x0, matrix products: 10.2 us -> none  [the longest x10 8.87 us: shards(): jnp.dot(stacked[source], dec_weight[pair_index], preferred_element_type=j...]
    pallas_call x0 -> x3, Pallas kernels: none -> 8.43 us  [the longest x1 6.18 us: shards(): pl.pallas_call(decode_kernel, out_shape=jax.ShapeDtypeStruct((layer_count...]
    all_to_all x0 -> x1, starting transfers between devices: none -> 7.25 us  [shards(): x = lax.all_to_all(spread, 'feat', 0, 0, tiled=True).reshape(tokens, width)]
    unnamed x25 -> x12, local copies, waits for them, and re-layouts: 20 us -> 13.5 us
  transfers between devices with their start and end apart: 1 -> 1, of which waited for: 1 -> 1; matrix products, arithmetic and copies ran while one was open for 0% -> 1% of each run, Pallas kernels for 0% -> 0%
where the time goes in v1:
time: 52.5 us; the launch traced here: 52 us
  blocking collectives  14.7 us (28%)
  local copies, waits for them, and re-layouts  14.1 us (27%)
  Pallas kernels  8.43 us (16%)
  starting transfers between devices  7.25 us (14%)
  waiting for transfers between devices  5.93 us (11%)
  other arithmetic  1.59 us (3%)
    unnamed x12, local copies, waits for them, and re-layouts  13.5 us
    all_to_all x1, blocking collectives, shards(): arrived = lax.all_to_all(parts, ('layer', 'feat'), 0, 0, tiled=True)  9.28 us
    all_to_all x1, starting transfers between devices, shards(): x = lax.all_to_all(spread, 'feat', 0, 0, tiled=True).reshape(tokens, width)  7.25 us
    pallas_call x1, Pallas kernels, shards(): pl.pallas_call(decode_kernel, out_shape=jax.ShapeDtypeStruct((layer_count...  6.18 us
    all_to_all x1, waiting for transfers between devices, shards(): x = lax.all_to_all(spread, 'feat', 0, 0, tiled=True).reshape(tokens, width)  5.93 us
    all_gather x1, blocking collectives, shards(): stacked = lax.all_gather(latent[None], 'layer', axis=0, tiled=True)  5.42 us
    pallas_call x1, Pallas kernels, shards(): pl.pallas_call(encode_kernel, out_shape=jax.ShapeDtypeStruct((tokens, fea...  1.5 us
  transfers between devices with their start and end apart: 1, of which 1 were waited for; matrix products, arithmetic and copies ran while one was open for 1% of the time, Pallas kernels for 0%

profile of v1, /device:TPU:0, one launch (start us, length us, event | category | flops | bytes accessed | tf_op | source)
XLA Modules:
  0.0 52.0 jit_solution(4733706818506489618)
XLA Ops:
  0.0 0.0 copy-start.2
  0.0 0.7 %reduce = bf16[2304]{0:T(1024)(128)(2,1)S(1)} reduce(bf16[1,1,2304]{2,1,0:T(2,128)(2,1)} %param.6, bf16[]{:T(256)} %constant.5), dimensions={0,1}, to_apply=%param.6.reduce_sub_computation | reduce | bytes 9218 | tf_op args[0]
  0.8 0.5 broadcast.3
  1.3 0.8 %reduce.1 = bf16[8,2304]{1,0:T(8,128)(2,1)S(1)} reduce(bf16[8,1,2304]{2,1,0:T(2,128)(2,1)S(1)} %reshape.10, bf16[]{:T(256)} %broadcast.3), dimensions={1}, to_apply=%reshape.10.reduce_sub_computation | reduce | bytes 73730 | tf_op jit(solution)/shard_map/reshape | solution.py:68
  2.2 0.6 %reshape.15 = bf16[8,2,1152]{2,1,0:T(2,128)(2,1)} reshape(bf16[8,2304]{1,0:T(8,128)(2,1)S(1)} %reduce.1) | data formatting | bytes 73728
  2.8 7.3 %all-to-all-start = ((bf16[8,2,1152]{2,1,0:T(2,128)(2,1)}), bf16[8,2,1152]{2,1,0:T(2,128)(2,1)S(1)}, u32[]{:S(2)}, u32[]{:S(2)}) async-start(bf16[8,2,1152]{2,1,0:T(2,128)(2,1)} %reshape.15), calls=%async_computation | async-start | bytes 73728 | tf_op jit(solution)/shard_map/all_to_all | solution.py:69
  10.1 0.8 %copy.9 = s32[1,18,16]{2,1,0:T(8,128)S(1)} copy(s32[1,18,16]{1,2,0:T(8,128)} %param.8) | data formatting | bytes 2304 | tf_op args[2]
  10.8 5.9 %all-to-all-done = bf16[8,2,1152]{2,1,0:T(2,128)(2,1)S(1)} async-done(((bf16[8,2,1152]{2,1,0:T(2,128)(2,1)}), bf16[8,2,1152]{2,1,0:T(2,128)(2,1)S(1)}, u32[]{:S(2)}, u32[]{:S(2)}) %all-to-all-start) | async-done | bytes 36896 | tf_op jit(solution)/shard_map/all_to_all | solution.py:69
  16.8 0.0 copy-start.1
  16.8 3.7 %copy-done.1 = bf16[1,2304,2048]{2,1,0:T(8,128)(2,1)S(1)} copy-done((bf16[1,2304,2048]{2,1,0:T(8,128)(2,1)S(1)}, bf16[1,2304,2048]{2,1,0:T(8,128)(2,1)}, u32[]{:S(2)}) %copy-start.1) | copy-done | bytes 9437208
  20.5 0.0 copy-start.3
  20.5 0.7 %copy-done.3 = f32[1,2048]{1,0:T(1,128)S(1)} copy-done((f32[1,2048]{1,0:T(1,128)S(1)}, f32[1,2048]{1,0:T(1,128)}, u32[]{:S(2)}) %copy-start.3) | copy-done | bytes 8216
  21.2 1.5 %encode.1 = bf16[8,2048]{1,0:T(8,128)(2,1)S(1)} custom-call(bf16[8,2304]{1,0:T(8,128)(2,1)S(1)} %bitcast.12, bf16[2304,2048]{1,0:T(8,128)(2,1)S(1)} %bitcast.9, s32[18,16]{1,0:T(8,128)S(1)} %bitcast.13, f32[1,2048]{1,0:T(1,128)S(1)} %copy-done.3), custom_call_target="tpu_custom_call" | custom-call | tf_op jit(solution)/shard_map/encode/pallas_call | solution.py:70
  22.7 5.4 %all-gather = bf16[32,2048]{1,0:T(8,128)(2,1)S(1)} all-gather(bf16[8,2048]{1,0:T(8,128)(2,1)S(1)} %encode.1), channel_id=2, replica_groups=mesh['layer'=4,'feat'=8] {'layer'}, dimensions={0}, use_global_device_ids=true | all-gather | bytes 163840 | tf_op jit(solution)/shard_map/all_gather | solution.py:78
  28.1 0.0 copy-start
  28.1 7.7 %copy-done = bf16[10,2048,576]{1,2,0:T(8,128)(2,1)S(1)} copy-done((bf16[10,2048,576]{1,2,0:T(8,128)(2,1)S(1)}, bf16[10,2048,576]{1,2,0:T(8,128)(2,1)}, u32[]{:S(2)}) %copy-start) | copy-done | bytes 23592984
  35.8 6.2 %decode.1 = f32[32,1,576]{2,1,0:T(1,128)S(1)} custom-call(bf16[4,8,2048]{2,1,0:T(8,128)(2,1)S(1)} %bitcast.10, bf16[10,576,2048]{2,1,0:T(8,128)(2,1)S(1)} %bitcast.8), custom_call_target="tpu_custom_call" | custom-call | tf_op jit(solution)/shard_map/decode/pallas_call | solution.py:79
  42.0 9.3 %all_to_all.10 = f32[32,1,576]{2,1,0:T(1,128)S(1)} all-to-all(f32[32,1,576]{2,1,0:T(1,128)S(1)} %decode.1), channel_id=1, replica_groups=mesh['layer'=4,'feat'=8] {'layer','feat'}, dimensions={0} | all-to-all | bytes 147456 | tf_op jit(solution)/shard_map/all_to_all | solution.py:87
  51.3 0.0 copy-done.2
  51.3 0.7 %finish.1 = bf16[1,1,2304]{2,1,0:T(2,128)(2,1)} custom-call(f32[4,8,1,576]{3,2,1,0:T(1,128)S(1)} %bitcast.11, f32[1,2304]{1,0:T(1,128)S(1)} %copy-done.2), custom_call_target="tpu_custom_call" | custom-call | tf_op jit(solution)/shard_map/finish/pallas_call | solution.py:88
  (3 shorter events, 0.1 us)
Async XLA Ops:
  0.0 51.3 %copy-start.2 = (f32[1,2304]{1,0:T(1,128)S(1)}, f32[1,2304]{1,0:T(1,128)}, u32[]{:S(2)}) copy-start(f32[1,2304]{1,0:T(1,128)} %bias_ref.3) | copy-start | bytes 27652
  2.8 14.0 %all-to-all-start = ((bf16[8,2,1152]{2,1,0:T(2,128)(2,1)}), bf16[8,2,1152]{2,1,0:T(2,128)(2,1)S(1)}, u32[]{:S(2)}, u32[]{:S(2)}) async-start(bf16[8,2,1152]{2,1,0:T(2,128)(2,1)} %reshape.15), calls=%async_computation | async-start | bytes 73728 | tf_op jit(solution)/shard_map/all_to_all | solution.py:69
  16.8 3.7 %copy-start.1 = (bf16[1,2304,2048]{2,1,0:T(8,128)(2,1)S(1)}, bf16[1,2304,2048]{2,1,0:T(8,128)(2,1)}, u32[]{:S(2)}) copy-start(bf16[1,2304,2048]{2,1,0:T(8,128)(2,1)} %param.7) | copy-start | bytes 28311556
  20.5 0.7 %copy-start.3 = (f32[1,2048]{1,0:T(1,128)S(1)}, f32[1,2048]{1,0:T(1,128)}, u32[]{:S(2)}) copy-start(f32[1,2048]{1,0:T(1,128)} %bias_ref.2) | copy-start | bytes 24580
  28.1 7.7 %copy-start = (bf16[10,2048,576]{1,2,0:T(8,128)(2,1)S(1)}, bf16[10,2048,576]{1,2,0:T(8,128)(2,1)}, u32[]{:S(2)}) copy-start(bf16[10,2048,576]{1,2,0:T(8,128)(2,1)} %param.10) | copy-start | bytes 70778880

commit v2 on v1

--- a/solution.py
+++ b/solution.py
@@ -6,19 +6,31 @@
 from jax.sharding import PartitionSpec as P
 
 BLK = 128
+AXES = ("layer", "feat")
 VMEM = pl.BlockSpec(memory_space=pltpu.VMEM)
-LIMIT = 12 * 1024 * 1024
+LIMIT = 8 * 1024 * 1024
+WORK = 20_000_000_000
+OVER_ROWS = (((1,), (1,)), ((), ()))
 
 
-def encode_kernel(x_ref, mantissa_ref, exponent_ref, bias_ref, latent_ref):
-    x = x_ref[...].astype(jnp.float32)
+def cost(flops):
+    return pl.CostEstimate(flops=flops, bytes_accessed=0, transcendentals=0)
+
+
+def prepare_kernel(own_ref, copies_ref):
+    own = own_ref[0].astype(jnp.float32)
+    for copy in range(copies_ref.shape[0]):
+        copies_ref[copy] = own
+
+
+def encode_kernel(all_ref, mantissa_ref, exponent_ref, bias_ref, latent_ref):
+    x = all_ref[:, 0, :]
     tokens, width = x.shape
-    features = mantissa_ref.shape[1]
-    rows, blocks = exponent_ref.shape
+    blocks, rows = exponent_ref.shape
     scale = jnp.exp2(exponent_ref[...].astype(jnp.float32)).astype(jnp.bfloat16)
     row_of = lax.broadcasted_iota(jnp.int32, (rows, width), 1) // BLK
     spread = (row_of == lax.broadcasted_iota(jnp.int32, (rows, width), 0)).astype(jnp.bfloat16)
-    scales = lax.dot_general(scale, spread, (((0,), (0,)), ((), ())), preferred_element_type=jnp.float32)
+    scales = jnp.dot(scale, spread, preferred_element_type=jnp.float32)
     for first in range(0, blocks, 2):
         group = range(first, min(first + 2, blocks))
         scaled = jnp.concatenate([x * scales[j : j + 1, :] for j in group], axis=0).astype(jnp.bfloat16)
@@ -30,21 +42,23 @@
             latent_ref[:, there] = jnp.maximum(own + bias_ref[:, there], 0.0).astype(latent_ref.dtype)
 
 
-def decode_kernel(latent_ref, weight_ref, out_ref):
-    layers, tokens, _ = latent_ref.shape
+def decode_kernel(near_ref, far_ref, weight_ref, out_ref):
+    layer, shard = lax.axis_index("layer"), lax.axis_index("feat")
+    half, tokens, _ = near_ref.shape
+    layers = 2 * half
+    out_rows = out_ref.shape[0] // layers
+    latents = []
+    for source in range(layers):
+        slot = layer ^ source
+        latents.append(jnp.where(slot < half, near_ref[slot % half], far_ref[slot % half]))
     for target in range(layers):
         total = None
         for source in range(target + 1):
             pair = target * (target + 1) // 2 + source
-            part = lax.dot_general(
-                latent_ref[source],
-                weight_ref[pair],
-                (((1,), (1,)), ((), ())),
-                preferred_element_type=jnp.float32,
-            )
+            part = lax.dot_general(latents[source], weight_ref[pair], OVER_ROWS, preferred_element_type=jnp.float32)
             total = part if total is None else total + part
         for token in range(tokens):
-            out_ref[target * tokens + token] = total[token : token + 1, :]
+            out_ref[target * out_rows + token] = total[token : token + 1, :]
 
 
 def finish_kernel(parts_ref, bias_ref, out_ref):
@@ -65,26 +79,49 @@
     col_local = dec_weight.shape[2]
     params = pltpu.CompilerParams(vmem_limit_bytes=LIMIT)
 
-    spread = jnp.broadcast_to(resid_stream, (feat_count, tok_local, 1, width)).reshape(tokens, 1, width)
-    x = lax.all_to_all(spread, "feat", 0, 0, tiled=True).reshape(tokens, width)
+    def place(layer, feat):
+        return layer * feat_count + feat
+
+    everywhere = [(layer, feat) for layer in range(layer_count) for feat in range(feat_count)]
+
+    def swap(array, layer_bit=0, feat_bit=0, parities=(0, 1)):
+        return lax.ppermute(
+            array,
+            AXES,
+            [(place(l, f), place(l ^ layer_bit, f ^ feat_bit)) for l, f in everywhere if l % 2 in parities],
+        )
+
+    copies = pl.pallas_call(
+        prepare_kernel,
+        out_shape=jax.ShapeDtypeStruct((tokens, 1, width), jnp.float32),
+        in_specs=[VMEM],
+        out_specs=VMEM,
+        compiler_params=params,
+        cost_estimate=cost(WORK),
+        name="prepare",
+    )(resid_stream)
+    gathered = lax.all_to_all(copies, "feat", 0, 0, tiled=True)
     latent = pl.pallas_call(
         encode_kernel,
         out_shape=jax.ShapeDtypeStruct((tokens, feat_local), jnp.bfloat16),
         in_specs=[VMEM] * 4,
         out_specs=VMEM,
         compiler_params=params,
+        cost_estimate=cost(WORK),
         name="encode",
-    )(x, enc_mantissa[0], enc_exponent[0], enc_bias)
-    stacked = lax.all_gather(latent[None], "layer", axis=0, tiled=True)
+    )(gathered, enc_mantissa[0], jnp.swapaxes(enc_exponent[0], 0, 1), enc_bias)
+    near = jnp.stack([latent, swap(latent, layer_bit=1)])
+    far = swap(near, layer_bit=2)
     parts = pl.pallas_call(
         decode_kernel,
         out_shape=jax.ShapeDtypeStruct((layer_count * tokens, 1, col_local), jnp.float32),
-        in_specs=[VMEM] * 2,
+        in_specs=[VMEM] * 3,
         out_specs=VMEM,
         compiler_params=params,
+        cost_estimate=cost(WORK),
         name="decode",
-    )(stacked, jnp.swapaxes(dec_weight, 1, 2))
-    arrived = lax.all_to_all(parts, ("layer", "feat"), 0, 0, tiled=True)
+    )(near, far, jnp.swapaxes(dec_weight, 1, 2))
+    arrived = lax.all_to_all(parts, AXES, 0, 0, tiled=True)
     return pl.pallas_call(
         finish_kernel,
         out_shape=jax.ShapeDtypeStruct((tok_local, 1, width), jnp.bfloat16),

time: 52.5 us -> 39 us (0.74)
  local copies, waits for them, and re-layouts: 14.1 us -> 0.9 us
  blocking collectives: 14.7 us -> 23.7 us
  starting transfers between devices: 7.25 us -> 1.65 us
  waiting for transfers between devices: 5.93 us -> 3.94 us
  other arithmetic: 1.59 us -> 0.01 us
    all_to_all x1 -> x2, blocking collectives: 9.28 us -> 23.7 us  [the longest x1 14.3 us: shards(): gathered = lax.all_to_all(copies, 'feat', 0, 0, tiled=True)]
    unnamed x12 -> x22, local copies, waits for them, and re-layouts: 13.5 us -> 0.9 us
    all_to_all x1 -> x0, starting transfers between devices: 7.25 us -> none  [shards(): x = lax.all_to_all(spread, 'feat', 0, 0, tiled=True).reshape(tokens, width)]
    all_to_all x1 -> x0, waiting for transfers between devices: 5.93 us -> none  [shards(): x = lax.all_to_all(spread, 'feat', 0, 0, tiled=True).reshape(tokens, width)]
    all_gather x1 -> x0, blocking collectives: 5.42 us -> none  [shards(): stacked = lax.all_gather(latent[None], 'layer', axis=0, tiled=True)]
    ppermute x0 -> x2, waiting for transfers between devices: none -> 3.94 us  [swap(): lax.ppermute(array, AXES, [(place(l, f), place(l ^ layer_bit, f ^ feat_bi...]
    ppermute x0 -> x2, starting transfers between devices: none -> 1.65 us  [swap(): lax.ppermute(array, AXES, [(place(l, f), place(l ^ layer_bit, f ^ feat_bi...]
    reshape x1 -> x0, other arithmetic: 0.85 us -> none  [shards(): jnp.broadcast_to(resid_stream, (feat_count, tok_local, 1, width))]
  transfers between devices with their start and end apart: 1 -> 2, of which waited for: 1 -> 2; matrix products, arithmetic and copies ran while one was open for 1% -> 0% of each run, Pallas kernels for 0% -> 0%
where the time goes in v2:
time: 39 us; the launch traced here: 38.7 us
  blocking collectives  23.7 us (61%)
  Pallas kernels  8.41 us (22%)
  waiting for transfers between devices  3.94 us (10%)
  starting transfers between devices  1.65 us (4%)
  local copies, waits for them, and re-layouts  0.9 us (2%)
    all_to_all x1, blocking collectives, shards(): gathered = lax.all_to_all(copies, 'feat', 0, 0, tiled=True)  14.3 us
    all_to_all x1, blocking collectives, shards(): arrived = lax.all_to_all(parts, AXES, 0, 0, tiled=True)  9.43 us
    pallas_call x1, Pallas kernels, shards(): pl.pallas_call(decode_kernel, out_shape=jax.ShapeDtypeStruct((layer_count...  6.19 us
    ppermute x2, waiting for transfers between devices, swap(): lax.ppermute(array, AXES, [(place(l, f), place(l ^ layer_bit, f ^ feat_bi...  3.94 us
    ppermute x2, starting transfers between devices, swap(): lax.ppermute(array, AXES, [(place(l, f), place(l ^ layer_bit, f ^ feat_bi...  1.65 us
    pallas_call x1, Pallas kernels, shards(): pl.pallas_call(encode_kernel, out_shape=jax.ShapeDtypeStruct((tokens, fea...  1.46 us
    unnamed x22, local copies, waits for them, and re-layouts  0.9 us
  transfers between devices with their start and end apart: 2, of which 2 were waited for; matrix products, arithmetic and copies ran while one was open for 0% of the time, Pallas kernels for 0%

profile of v2, /device:TPU:0, one launch (start us, length us, event | category | flops | bytes accessed | tf_op | source)
XLA Modules:
  0.0 38.7 jit_solution(2124667897711567993)
XLA Ops:
  0.0 0.0 copy-start.1
  0.0 0.0 copy-start.2
  0.0 0.8 %copy-done.2 = bf16[1,1,2304]{2,1,0:T(2,128)(2,1)S(1)} copy-done((bf16[1,1,2304]{2,1,0:T(2,128)(2,1)S(1)}, bf16[1,1,2304]{2,1,0:T(2,128)(2,1)}, u32[]{:S(2)}) %copy-start.2) | copy-done | bytes 4632
  0.9 0.0 copy-start.3
  0.9 0.0 copy-start.4
  0.9 0.0 slice-start
  0.9 0.0 slice-start.1
  0.9 0.0 slice-start.2
  0.9 0.0 slice-start.3
  0.9 14.3 %all_to_all.10.all_ref = f32[8,1,2304]{2,1,0:T(1,128)S(1)} all-to-all(f32[8,1,2304]{2,1,0:T(1,128)S(1)} %prepare.1), channel_id=1, replica_groups=mesh['layer'=4,'feat'=8] {'feat'}, dimensions={0} | all-to-all | bytes 147456 | tf_op jit(solution)/shard_map/all_to_all | solution.py:103
  15.2 0.0 copy-done.1
  15.2 0.0 copy-done.3
  15.2 0.0 copy-done.4
  15.2 0.0 slice-start.4
  15.2 0.0 slice-start.5
  15.2 1.5 %encode.1 = bf16[8,2048]{1,0:T(8,128)(2,1)S(1)} custom-call(f32[8,1,2304]{2,1,0:T(1,128)S(1)} %all_to_all.10.all_ref, bf16[2304,2048]{1,0:T(8,128)(2,1)S(1)} %bitcast.13, s32[16,18]{1,0:T(8,128)S(1)} %bitcast.14, f32[1,2048]{1,0:T(1,128)S(1)} %copy-done.4), custom_call_target="tpu_custom_call" | custom-call | flops 20000000000 | tf_op jit(solution)/shard_map/encode/pallas_call | solution.py:104
  16.7 0.1 collective-permute-start
  16.8 1.2 %collective-permute-done = bf16[8,2048]{1,0:T(8,128)(2,1)S(1)} collective-permute-done((bf16[8,2048]{1,0:T(8,128)(2,1)S(1)}, bf16[8,2048]{1,0:T(8,128)(2,1)S(1)}, u32[]{:S(2)}, u32[]{:S(2)}) %collective-permute-start) | collective-permute-done | bytes 32800 | tf_op jit(solution)/shard_map/ppermute | solution.py:88
  18.0 1.6 %collective-permute-start.1 = (bf16[2,8,2048]{2,1,0:T(8,128)(2,1)S(1)}, bf16[2,8,2048]{2,1,0:T(8,128)(2,1)S(1)}, u32[]{:S(2)}, u32[]{:S(2)}) collective-permute-start(bf16[2,8,2048]{2,1,0:T(8,128)(2,1)S(1)} %pad_maximum_fusion.near_ref), channel_id=1, source_target_pairs={{0,16},{1,17},{2,18},{3,19},{4,20},{5,21},{6,22},{7,23},{8,24},{9,... | collective-permute-start | bytes 196616 | tf_op jit(solution)/shard_map/ppermute | solution.py:88
  19.5 2.7 %collective-permute-done.1.far_ref = bf16[2,8,2048]{2,1,0:T(8,128)(2,1)S(1)} collective-permute-done((bf16[2,8,2048]{2,1,0:T(8,128)(2,1)S(1)}, bf16[2,8,2048]{2,1,0:T(8,128)(2,1)S(1)}, u32[]{:S(2)}, u32[]{:S(2)}) %collective-permute-start.1) | collective-permute-done | bytes 65568 | tf_op jit(solution)/shard_map/ppermute | solution.py:88
  22.3 0.0 slice-done
  22.3 0.0 slice-done.1
  22.3 0.0 slice-done.2
  22.3 0.0 slice-done.3
  22.3 0.0 slice-done.4
  22.3 0.0 slice-done.5
  22.3 0.0 copy-start
  22.4 6.2 %decode.1 = f32[32,1,576]{2,1,0:T(1,128)S(1)} custom-call(bf16[2,8,2048]{2,1,0:T(8,128)(2,1)S(1)} %pad_maximum_fusion.near_ref, bf16[2,8,2048]{2,1,0:T(8,128)(2,1)S(1)} %collective-permute-done.1.far_ref, bf16[10,576,2048]{2,1,0:T(8,128)(2,1)S(1)} %bitcast.12), custom_call_target="tpu_custom_call" | custom-call | flops 20000000000 | tf_op jit(solution)/shard_map/decode/pallas_call | solution.py:115
  28.5 9.4 %all_to_all.11 = f32[32,1,576]{2,1,0:T(1,128)S(1)} all-to-all(f32[32,1,576]{2,1,0:T(1,128)S(1)} %decode.1), channel_id=1, replica_groups=mesh['layer'=4,'feat'=8] {'layer','feat'}, dimensions={0} | all-to-all | bytes 147456 | tf_op jit(solution)/shard_map/all_to_all | solution.py:124
  38.0 0.0 copy-done
  38.0 0.7 %finish.1 = bf16[1,1,2304]{2,1,0:T(2,128)(2,1)} custom-call(f32[4,8,1,576]{3,2,1,0:T(1,128)S(1)} %bitcast.8, f32[1,2304]{1,0:T(1,128)S(1)} %copy-done), custom_call_target="tpu_custom_call" | custom-call | tf_op jit(solution)/shard_map/finish/pallas_call | solution.py:125
  (3 shorter events, 0.0 us)
Async XLA Ops:
  0.0 15.2 %copy-start.1 = (bf16[1,2304,2048]{2,1,0:T(8,128)(2,1)S(1)}, bf16[1,2304,2048]{2,1,0:T(8,128)(2,1)}, u32[]{:S(2)}) copy-start(bf16[1,2304,2048]{2,1,0:T(8,128)(2,1)} %param.7) | copy-start | bytes 28311556
  0.0 0.8 %copy-start.2 = (bf16[1,1,2304]{2,1,0:T(2,128)(2,1)S(1)}, bf16[1,1,2304]{2,1,0:T(2,128)(2,1)}, u32[]{:S(2)}) copy-start(bf16[1,1,2304]{2,1,0:T(2,128)(2,1)} %own_ref.1) | copy-start | bytes 13828
  0.9 14.3 %copy-start.3 = (s32[1,18,16]{1,2,0:T(8,128)S(1)}, s32[1,18,16]{1,2,0:T(8,128)}, u32[]{:S(2)}) copy-start(s32[1,18,16]{1,2,0:T(8,128)} %param.8) | copy-start | bytes 3460
  0.9 14.3 %copy-start.4 = (f32[1,2048]{1,0:T(1,128)S(1)}, f32[1,2048]{1,0:T(1,128)}, u32[]{:S(2)}) copy-start(f32[1,2048]{1,0:T(1,128)} %bias_ref.2) | copy-start | bytes 24580
  0.9 21.4 %slice-start = ((s8[23592960]{0:T(1024)(128)(4,1)}), s8[4194304]{0:T(1024)(128)(4,1)S(1)}, s32[]{:S(2)}) async-start(s8[23592960]{0:T(1024)(128)(4,1)} %bitcast.10), calls=%async_computation.2 | async-start | bytes 8388608
  0.9 21.4 %slice-start.1 = ((s8[23592960]{0:T(1024)(128)(4,1)}), s8[4194304]{0:T(1024)(128)(4,1)S(1)}, s32[]{:S(2)}) async-start(s8[23592960]{0:T(1024)(128)(4,1)} %bitcast.10), calls=%async_computation.3 | async-start | bytes 8388608
  0.9 21.4 %slice-start.2 = ((s8[23592960]{0:T(1024)(128)(4,1)}), s8[4194304]{0:T(1024)(128)(4,1)S(1)}, s32[]{:S(2)}) async-start(s8[23592960]{0:T(1024)(128)(4,1)} %bitcast.10), calls=%async_computation.4 | async-start | bytes 8388608
  0.9 21.4 %slice-start.3 = ((s8[23592960]{0:T(1024)(128)(4,1)}), s8[4194304]{0:T(1024)(128)(4,1)S(1)}, s32[]{:S(2)}) async-start(s8[23592960]{0:T(1024)(128)(4,1)} %bitcast.10), calls=%async_computation.5 | async-start | bytes 8388608
  15.2 7.1 %slice-start.4 = ((s8[23592960]{0:T(1024)(128)(4,1)}), s8[4194304]{0:T(1024)(128)(4,1)S(1)}, s32[]{:S(2)}) async-start(s8[23592960]{0:T(1024)(128)(4,1)} %bitcast.10), calls=%async_computation.6 | async-start | bytes 8388608
  15.2 7.1 %slice-start.5 = ((s8[23592960]{0:T(1024)(128)(4,1)}), s8[2621440]{0:T(1024)(128)(4,1)S(1)}, s32[]{:S(2)}) async-start(s8[23592960]{0:T(1024)(128)(4,1)} %bitcast.10), calls=%async_computation.7 | async-start | bytes 5242880
  16.7 1.3 %collective-permute-start = (bf16[8,2048]{1,0:T(8,128)(2,1)S(1)}, bf16[8,2048]{1,0:T(8,128)(2,1)S(1)}, u32[]{:S(2)}, u32[]{:S(2)}) collective-permute-start(bf16[8,2048]{1,0:T(8,128)(2,1)S(1)} %encode.1), channel_id=1, source_target_pairs={{0,8},{1,9},{2,10},{3,11},{4,12},{5,13},{6,14},{7,15},{8,0},{9,1},... | collective-permute-start | bytes 98312 | tf_op jit(solution)/shard_map/ppermute | solution.py:88
  18.0 4.3 %collective-permute-start.1 = (bf16[2,8,2048]{2,1,0:T(8,128)(2,1)S(1)}, bf16[2,8,2048]{2,1,0:T(8,128)(2,1)S(1)}, u32[]{:S(2)}, u32[]{:S(2)}) collective-permute-start(bf16[2,8,2048]{2,1,0:T(8,128)(2,1)S(1)} %pad_maximum_fusion.near_ref), channel_id=1, source_target_pairs={{0,16},{1,17},{2,18},{3,19},{4,20},{5,21},{6,22},{7,23},{8,24},{9,... | collective-permute-start | bytes 196616 | tf_op jit(solution)/shard_map/ppermute | solution.py:88
  22.3 15.6 %copy-start = (f32[1,2304]{1,0:T(1,128)S(1)}, f32[1,2304]{1,0:T(1,128)}, u32[]{:S(2)}) copy-start(f32[1,2304]{1,0:T(1,128)} %bias_ref.3) | copy-start | bytes 27652

commit v3 on v2

v3 whole, which is shorter than its diff:
```python
import functools

import jax
import jax.numpy as jnp
from jax import lax
from jax.experimental import pallas as pl
from jax.experimental.pallas import tpu as pltpu
from jax.sharding import PartitionSpec as P

BLK = 128
AXES = ("layer", "feat")
VMEM = pl.BlockSpec(memory_space=pltpu.VMEM)
LIMIT = 8 * 1024 * 1024
WORK = 20_000_000_000
OVER_ROWS = (((1,), (1,)), ((), ()))


def kernel(body, out_shape, name, scratch_shapes=()):
    def call(*operands):
        return pl.pallas_call(
            body,
            out_shape=out_shape,
            in_specs=[VMEM] * len(operands),
            out_specs=VMEM,
            scratch_shapes=scratch_shapes,
            compiler_params=pltpu.CompilerParams(vmem_limit_bytes=LIMIT),
            cost_estimate=pl.CostEstimate(flops=WORK, bytes_accessed=0, transcendentals=0),
            name=name,
        )(*operands)

    return call


def prepare_kernel(own_ref, copies_ref):
    own = own_ref[0].astype(jnp.float32)
    for copy in range(copies_ref.shape[0]):
        copies_ref[copy] = own


def encode_kernel(all_ref, mantissa_ref, exponent_ref, bias_ref, latent_ref):
    x = all_ref[:, 0, :]
    tokens, width = x.shape
    blocks, rows = exponent_ref.shape
    scale = jnp.exp2(exponent_ref[...].astype(jnp.float32)).astype(jnp.bfloat16)
    row_of = lax.broadcasted_iota(jnp.int32, (rows, width), 1) // BLK
    spread = (row_of == lax.broadcasted_iota(jnp.int32, (rows, width), 0)).astype(jnp.bfloat16)
    scales = jnp.dot(scale, spread, preferred_element_type=jnp.float32)
    for first in range(0, blocks, 2):
        group = range(first, min(first + 2, blocks))
        scaled = jnp.concatenate([x * scales[j : j + 1, :] for j in group], axis=0).astype(jnp.bfloat16)
        columns = slice(first * BLK, (first + len(group)) * BLK)
        product = jnp.dot(scaled, mantissa_ref[:, columns], preferred_element_type=jnp.float32)
        for at, j in enumerate(group):
            own = product[at * tokens : (at + 1) * tokens, at * BLK : (at + 1) * BLK]
            there = slice(j * BLK, (j + 1) * BLK)
            latent_ref[:, there] = jnp.maximum(own + bias_ref[:, there], 0.0).astype(latent_ref.dtype)


def product(latent, weight_ref, pair):
    columns, features = weight_ref.shape[1:]
    still, step = columns // 512 * 256, min(features, 256)
    fixed, moved = None, None
    for at in range(0, features, step):
        there = slice(at, at + step)
        if still:
            part = lax.dot_general(
                latent[:, there], weight_ref[pair, :still, there], OVER_ROWS, preferred_element_type=jnp.float32
            )
            fixed = part if fixed is None else fixed + part
        part = lax.dot_general(
            weight_ref[pair, still:, there], latent[:, there], OVER_ROWS, preferred_element_type=jnp.float32
        )
        moved = part if moved is None else moved + part
    return jnp.concatenate([fixed, moved.T], axis=1) if still else moved.T


def add_pair(total_ref, latent, weight_ref, source, target):
    total_ref[target] += product(latent, weight_ref, target * (target + 1) // 2 + source)


def decode_own_kernel(own_ref, weight_ref, total_ref):
    layer, layers = lax.axis_index("layer"), total_ref.shape[0]
    total_ref[...] = jnp.zeros_like(total_ref)

    count = layers - layer

    @pl.when(count % 2 == 1)
    def _():
        add_pair(total_ref, own_ref[...], weight_ref, layer, layer)

    for first in range(0, layers, 2):

        @pl.when(first + 2 <= count)
        def _():
            for at in (first, first + 1):
                add_pair(total_ref, own_ref[...], weight_ref, layer, layer + count % 2 + at)


def decode_far_kernel(parity, total_ref, far_ref, weight_ref, out_ref):
    layer, layers = lax.axis_index("layer"), total_ref.shape[0]
    out_ref[...] = total_ref[...]
    source = layer ^ 2
    count = jnp.where(layer % 2 == parity, layers - source, 0)

    @pl.when(count % 2 == 1)
    def _():
        add_pair(out_ref, far_ref[...], weight_ref, source, source)

    for first in range(0, layers, 2):

        @pl.when(first + 2 <= count)
        def _():
            for at in (first, first + 1):
                add_pair(out_ref, far_ref[...], weight_ref, source, source + count % 2 + at)


def decode_last_kernel(total_ref, both_ref, weight_ref, out_ref, sum_ref):
    layer, layers = lax.axis_index("layer"), total_ref.shape[0]
    tokens = both_ref.shape[1]
    sum_ref[...] = total_ref[...]
    sources = (layer ^ 1, layer ^ 3)
    first_count = layers - sources[0]
    count = first_count + layers - sources[1]

    def step(at):
        at_first = at < first_count
        source = jnp.where(at_first, sources[0], sources[1])
        target = jnp.where(at_first, sources[0] + at, sources[1] + at - first_count)
        add_pair(sum_ref, both_ref[jnp.where(at_first, 0, 1)], weight_ref, source, target)

    for at in range(layers):
        step(at)

    @pl.when(count > layers)
    def _():
        for at in (layers, layers + 1):
            step(at)

    for target in range(layers):
        total = sum_ref[target]
        for token in range(tokens):
            out_ref[target * tokens + token] = total[token : token + 1, :]


def finish_kernel(parts_ref, bias_ref, out_ref):
    layers, shards, columns = parts_ref.shape[0], parts_ref.shape[1], parts_ref.shape[3]
    for block in range(layers):
        there = slice(block * columns, (block + 1) * columns)
        total = parts_ref[block, 0]
        for shard in range(1, shards):
            total = total + parts_ref[block, shard]
        out_ref[:, 0, there] = (total + bias_ref[:, there]).astype(out_ref.dtype)


def shards(resid_stream, enc_mantissa, enc_exponent, enc_bias, dec_weight, dec_bias):
    layer_count, feat_count = lax.axis_size("layer"), lax.axis_size("feat")
    tok_local, _, width = resid_stream.shape
    tokens = tok_local * feat_count
    feat_local = enc_mantissa.shape[2]
    col_local = dec_weight.shape[2]

    def place(layer, feat):
        return layer * feat_count + feat

    everywhere = [(layer, feat) for layer in range(layer_count) for feat in range(feat_count)]

    def swap(array, layer_bit=0, feat_bit=0, parities=(0, 1)):
        return lax.ppermute(
            array,
            AXES,
            [(place(l, f), place(l ^ layer_bit, f ^ feat_bit)) for l, f in everywhere if l % 2 in parities],
        )

    copies = kernel(prepare_kernel, jax.ShapeDtypeStruct((tokens, 1, width), jnp.float32), "prepare")(resid_stream)
    gathered = lax.all_to_all(copies, "feat", 0, 0, tiled=True)
    latent = kernel(encode_kernel, jax.ShapeDtypeStruct((tokens, feat_local), jnp.bfloat16), "encode")(
        gathered, enc_mantissa[0], jnp.swapaxes(enc_exponent[0], 0, 1), enc_bias
    )
    weight = jnp.swapaxes(dec_weight, 1, 2)
    total = jax.ShapeDtypeStruct((layer_count, tokens, col_local), jnp.float32)
    far = swap(latent, layer_bit=2)
    own_total = kernel(decode_own_kernel, total, "decode_own")(latent, weight)
    odd_total = kernel(functools.partial(decode_far_kernel, 1), total, "decode_far_odd")(own_total, far, weight)
    held, odd_total = lax.optimization_barrier((jnp.stack([latent, far]), odd_total))
    both = swap(held, layer_bit=1)
    even_total = kernel(functools.partial(decode_far_kernel, 0), total, "decode_far_even")(odd_total, far, weight)
    parts = kernel(
        decode_last_kernel,
        jax.ShapeDtypeStruct((layer_count * tokens, 1, col_local), jnp.float32),
        "decode_last",
        scratch_shapes=[pltpu.VMEM(total.shape, total.dtype)],
    )(even_total, both, weight)
    arrived = lax.all_to_all(parts, AXES, 0, 0, tiled=True)
    return kernel(finish_kernel, jax.ShapeDtypeStruct((tok_local, 1, width), jnp.bfloat16), "finish")(
        arrived.reshape(layer_count, feat_count, tok_local, col_local), dec_bias
    )


def solution(mesh):
    in_specs = (
        P("feat", "layer", None),
        P("layer", None, "feat"),
        P("layer", None, "feat"),
        P("layer", "feat"),
        P(None, "feat", "layer"),
        P("layer", None),
    )
    out_specs = P("feat", "layer", None)
    return jax.shard_map(shards, mesh=mesh, in_specs=in_specs, out_specs=out_specs, check_vma=False)
```

time: 39 us -> 35.1 us (0.900)
  waiting for transfers between devices: 3.94 us -> 0.6 us
  Pallas kernels: 8.41 us -> 7.07 us
  blocking collectives: 23.7 us -> 24.5 us
    ppermute x2, waiting for transfers between devices: 3.94 us -> 0.6 us  [swap(): lax.ppermute(array, AXES, [(place(l, f), place(l ^ layer_bit, f ^ feat_bi...]
    pallas_call x4 -> x7, Pallas kernels: 8.41 us -> 7.07 us  [call(): pl.pallas_call(body, out_shape=out_shape, in_specs=[VMEM] * len(operands)...]
    all_to_all x1, blocking collectives: 9.43 us -> 10.2 us  [shards(): arrived = lax.all_to_all(parts, AXES, 0, 0, tiled=True)]
  transfers between devices with their start and end apart: 2 -> 2, of which waited for: 2 -> 2; matrix products, arithmetic and copies ran while one was open for 0% -> 0% of each run, Pallas kernels for 0% -> 9%
where the time goes in v3:
time: 35.1 us; the launch traced here: 34.8 us
  blocking collectives  24.5 us (70%)
  Pallas kernels  7.07 us (20%)
  starting transfers between devices  1.65 us (5%)
  local copies, waits for them, and re-layouts  0.9 us (3%)
  waiting for transfers between devices  0.6 us (2%)
    all_to_all x1, blocking collectives, shards(): gathered = lax.all_to_all(copies, 'feat', 0, 0, tiled=True)  14.3 us
    all_to_all x1, blocking collectives, shards(): arrived = lax.all_to_all(parts, AXES, 0, 0, tiled=True)  10.2 us
    pallas_call x7, Pallas kernels, call(): pl.pallas_call(body, out_shape=out_shape, in_specs=[VMEM] * len(operands)...  7.07 us
    ppermute x2, starting transfers between devices, swap(): lax.ppermute(array, AXES, [(place(l, f), place(l ^ layer_bit, f ^ feat_bi...  1.65 us
    unnamed x22, local copies, waits for them, and re-layouts  0.9 us
  transfers between devices with their start and end apart: 2, of which 2 were waited for; matrix products, arithmetic and copies ran while one was open for 0% of the time, Pallas kernels for 9%

profile of v3, /device:TPU:0, one launch (start us, length us, event | category | flops | bytes accessed | tf_op | source)
XLA Modules:
  0.0 34.8 jit_solution(16707257058584076877)
XLA Ops:
  0.0 0.0 copy-start
  0.0 0.0 copy-start.1
  0.0 0.8 %copy-done.1 = bf16[1,1,2304]{2,1,0:T(2,128)(2,1)S(1)} copy-done((bf16[1,1,2304]{2,1,0:T(2,128)(2,1)S(1)}, bf16[1,1,2304]{2,1,0:T(2,128)(2,1)}, u32[]{:S(2)}) %copy-start.1) | copy-done | bytes 4632
  0.9 0.0 copy-start.3
  0.9 0.0 copy-start.4
  0.9 0.0 slice-start
  0.9 0.0 slice-start.1
  0.9 0.0 slice-start.2
  0.9 0.0 slice-start.3
  0.9 14.3 %all_to_all.10.all_ref = f32[8,1,2304]{2,1,0:T(1,128)S(1)} all-to-all(f32[8,1,2304]{2,1,0:T(1,128)S(1)} %prepare.1), channel_id=1, replica_groups=mesh['layer'=4,'feat'=8] {'feat'}, dimensions={0} | all-to-all | bytes 147456 | tf_op jit(solution)/shard_map/all_to_all | solution.py:175
  15.2 0.0 copy-done
  15.2 0.0 copy-done.3
  15.2 0.0 copy-done.4
  15.2 0.0 slice-start.4
  15.2 0.0 slice-start.5
  15.2 1.5 %encode.1.own_ref = bf16[8,2048]{1,0:T(8,128)(2,1)S(1)} custom-call(f32[8,1,2304]{2,1,0:T(1,128)S(1)} %all_to_all.10.all_ref, bf16[2304,2048]{1,0:T(8,128)(2,1)S(1)} %bitcast.17, s32[16,18]{1,0:T(8,128)S(1)} %bitcast.18, f32[1,2048]{1,0:T(1,128)S(1)} %copy-done.4), custom_call_target="tpu_custom_call" | custom-call | flops 20000000000 | tf_op jit(solution)/shard_map/encode/pallas_call | solution.py:20
  16.7 1.6 %collective-permute-start = (bf16[8,2048]{1,0:T(8,128)(2,1)S(1)}, bf16[8,2048]{1,0:T(8,128)(2,1)S(1)}, u32[]{:S(2)}, u32[]{:S(2)}) collective-permute-start(bf16[8,2048]{1,0:T(8,128)(2,1)S(1)} %encode.1.own_ref), channel_id=1, source_target_pairs={{0,16},{1,17},{2,18},{3,19},{4,20},{5,21},{6,22},{7,23},{8,24},{9,... | collective-permute-start | bytes 98312 | tf_op jit(solution)/shard_map/ppermute | solution.py:168
  18.3 0.0 slice-done
  18.3 0.0 slice-done.1
  18.3 0.0 slice-done.2
  18.3 0.0 slice-done.3
  18.3 0.0 slice-done.4
  18.3 0.0 slice-done.5
  18.3 2.0 %decode_own.1.total_ref = f32[4,8,576]{2,1,0:T(8,128)S(1)} custom-call(bf16[8,2048]{1,0:T(8,128)(2,1)S(1)} %encode.1.own_ref, bf16[10,576,2048]{2,1,0:T(8,128)(2,1)S(1)} %bitcast.13), custom_call_target="tpu_custom_call" | custom-call | flops 20000000000 | tf_op jit(solution)/shard_map/decode_own/pallas_call | solution.py:20
  20.3 0.4 %collective-permute-done.far_ref = bf16[8,2048]{1,0:T(8,128)(2,1)S(1)} collective-permute-done((bf16[8,2048]{1,0:T(8,128)(2,1)S(1)}, bf16[8,2048]{1,0:T(8,128)(2,1)S(1)}, u32[]{:S(2)}, u32[]{:S(2)}) %collective-permute-start) | collective-permute-done | bytes 32800 | tf_op jit(solution)/shard_map/ppermute | solution.py:168
  20.7 0.1 collective-permute-start.1
  20.8 1.0 %decode_far_even.1.total_ref = f32[4,8,576]{2,1,0:T(8,128)S(1)} custom-call(f32[4,8,576]{2,1,0:T(8,128)S(1)} %decode_far_odd.1.total_ref, bf16[8,2048]{1,0:T(8,128)(2,1)S(1)} %collective-permute-done.far_ref, bf16[10,576,2048]{2,1,0:T(8,128)(2,1)S(1)} %bitcast.15), custom_call_target="tpu_custom_call" | custom-call | flops 20000000000 | tf_op jit(solution)/shard_map/decode_far_even/pallas_call | solution.py:20
  21.8 0.0 copy-start.2
  21.8 0.2 collective-permute-done.1.both_ref
  22.0 1.8 %decode_last.1 = f32[32,1,576]{2,1,0:T(1,128)S(1)} custom-call(f32[4,8,576]{2,1,0:T(8,128)S(1)} %decode_far_even.1.total_ref, bf16[2,8,2048]{2,1,0:T(8,128)(2,1)S(1)} %collective-permute-done.1.both_ref, bf16[10,576,2048]{2,1,0:T(8,128)(2,1)S(1)} %bitcast.16), custom_call_target="tpu_custom_call" | custom-call | flops 20000000000 | tf_op jit(solution)/shard_map/decode_last/pallas_call | solution.py:20
  23.9 10.2 %all_to_all.11 = f32[32,1,576]{2,1,0:T(1,128)S(1)} all-to-all(f32[32,1,576]{2,1,0:T(1,128)S(1)} %decode_last.1), channel_id=1, replica_groups=mesh['layer'=4,'feat'=8] {'layer','feat'}, dimensions={0} | all-to-all | bytes 147456 | tf_op jit(solution)/shard_map/all_to_all | solution.py:193
  34.1 0.0 copy-done.2
  34.1 0.7 %finish.1 = bf16[1,1,2304]{2,1,0:T(2,128)(2,1)} custom-call(f32[4,8,1,576]{3,2,1,0:T(1,128)S(1)} %bitcast.8, f32[1,2304]{1,0:T(1,128)S(1)} %copy-done.2), custom_call_target="tpu_custom_call" | custom-call | flops 20000000000 | tf_op jit(solution)/shard_map/finish/pallas_call | solution.py:20
  (4 shorter events, 0.1 us)
Async XLA Ops:
  0.0 15.2 %copy-start = (bf16[1,2304,2048]{2,1,0:T(8,128)(2,1)S(1)}, bf16[1,2304,2048]{2,1,0:T(8,128)(2,1)}, u32[]{:S(2)}) copy-start(bf16[1,2304,2048]{2,1,0:T(8,128)(2,1)} %param.7) | copy-start | bytes 28311556
  0.0 0.8 %copy-start.1 = (bf16[1,1,2304]{2,1,0:T(2,128)(2,1)S(1)}, bf16[1,1,2304]{2,1,0:T(2,128)(2,1)}, u32[]{:S(2)}) copy-start(bf16[1,1,2304]{2,1,0:T(2,128)(2,1)} %own_ref.1) | copy-start | bytes 13828
  0.9 14.3 %copy-start.3 = (s32[1,18,16]{1,2,0:T(8,128)S(1)}, s32[1,18,16]{1,2,0:T(8,128)}, u32[]{:S(2)}) copy-start(s32[1,18,16]{1,2,0:T(8,128)} %param.8) | copy-start | bytes 3460
  0.9 14.3 %copy-start.4 = (f32[1,2048]{1,0:T(1,128)S(1)}, f32[1,2048]{1,0:T(1,128)}, u32[]{:S(2)}) copy-start(f32[1,2048]{1,0:T(1,128)} %bias_ref.2) | copy-start | bytes 24580
  0.9 17.4 %slice-start = ((s8[23592960]{0:T(1024)(128)(4,1)}), s8[4194304]{0:T(1024)(128)(4,1)S(1)}, s32[]{:S(2)}) async-start(s8[23592960]{0:T(1024)(128)(4,1)} %bitcast.11), calls=%async_computation.2 | async-start | bytes 8388608
  0.9 17.4 %slice-start.1 = ((s8[23592960]{0:T(1024)(128)(4,1)}), s8[4194304]{0:T(1024)(128)(4,1)S(1)}, s32[]{:S(2)}) async-start(s8[23592960]{0:T(1024)(128)(4,1)} %bitcast.11), calls=%async_computation.3 | async-start | bytes 8388608
  0.9 17.4 %slice-start.2 = ((s8[23592960]{0:T(1024)(128)(4,1)}), s8[4194304]{0:T(1024)(128)(4,1)S(1)}, s32[]{:S(2)}) async-start(s8[23592960]{0:T(1024)(128)(4,1)} %bitcast.11), calls=%async_computation.4 | async-start | bytes 8388608
  0.9 17.4 %slice-start.3 = ((s8[23592960]{0:T(1024)(128)(4,1)}), s8[4194304]{0:T(1024)(128)(4,1)S(1)}, s32[]{:S(2)}) async-start(s8[23592960]{0:T(1024)(128)(4,1)} %bitcast.11), calls=%async_computation.5 | async-start | bytes 8388608
  15.2 3.1 %slice-start.4 = ((s8[23592960]{0:T(1024)(128)(4,1)}), s8[4194304]{0:T(1024)(128)(4,1)S(1)}, s32[]{:S(2)}) async-start(s8[23592960]{0:T(1024)(128)(4,1)} %bitcast.11), calls=%async_computation.6 | async-start | bytes 8388608
  15.2 3.1 %slice-start.5 = ((s8[23592960]{0:T(1024)(128)(4,1)}), s8[2621440]{0:T(1024)(128)(4,1)S(1)}, s32[]{:S(2)}) async-start(s8[23592960]{0:T(1024)(128)(4,1)} %bitcast.11), calls=%async_computation.7 | async-start | bytes 5242880
  16.7 4.0 %collective-permute-start = (bf16[8,2048]{1,0:T(8,128)(2,1)S(1)}, bf16[8,2048]{1,0:T(8,128)(2,1)S(1)}, u32[]{:S(2)}, u32[]{:S(2)}) collective-permute-start(bf16[8,2048]{1,0:T(8,128)(2,1)S(1)} %encode.1.own_ref), channel_id=1, source_target_pairs={{0,16},{1,17},{2,18},{3,19},{4,20},{5,21},{6,22},{7,23},{8,24},{9,... | collective-permute-start | bytes 98312 | tf_op jit(solution)/shard_map/ppermute | solution.py:168
  20.7 1.3 %collective-permute-start.1 = (bf16[2,8,2048]{2,1,0:T(8,128)(2,1)S(1)}, bf16[2,8,2048]{2,1,0:T(8,128)(2,1)S(1)}, u32[]{:S(2)}, u32[]{:S(2)}) collective-permute-start(bf16[2,8,2048]{2,1,0:T(8,128)(2,1)S(1)} %pad_maximum_fusion), channel_id=1, source_target_pairs={{0,8},{1,9},{2,10},{3,11},{4,12},{5,13},{6,14},{7,15},{8,0},{9,1},... | collective-permute-start | bytes 196616 | tf_op jit(solution)/shard_map/ppermute | solution.py:168
  21.8 12.3 %copy-start.2 = (f32[1,2304]{1,0:T(1,128)S(1)}, f32[1,2304]{1,0:T(1,128)}, u32[]{:S(2)}) copy-start(f32[1,2304]{1,0:T(1,128)} %bias_ref.3) | copy-start | bytes 27652

commit v4 on v3

--- a/solution.py
+++ b/solution.py
@@ -56,90 +56,74 @@
             latent_ref[:, there] = jnp.maximum(own + bias_ref[:, there], 0.0).astype(latent_ref.dtype)
 
 
-def product(latent, weight_ref, pair):
+def products(latents, weight_ref, target):
     columns, features = weight_ref.shape[1:]
     still, step = columns // 512 * 256, min(features, 256)
     fixed, moved = None, None
-    for at in range(0, features, step):
-        there = slice(at, at + step)
-        if still:
+    for source, latent in latents:
+        pair = target * (target + 1) // 2 + source
+        for at in range(0, features, step):
+            there = slice(at, at + step)
+            if still:
+                part = lax.dot_general(
+                    latent[:, there], weight_ref[pair, :still, there], OVER_ROWS, preferred_element_type=jnp.float32
+                )
+                fixed = part if fixed is None else fixed + part
             part = lax.dot_general(
-                latent[:, there], weight_ref[pair, :still, there], OVER_ROWS, preferred_element_type=jnp.float32
+                weight_ref[pair, still:, there], latent[:, there], OVER_ROWS, preferred_element_type=jnp.float32
             )
-            fixed = part if fixed is None else fixed + part
-        part = lax.dot_general(
-            weight_ref[pair, still:, there], latent[:, there], OVER_ROWS, preferred_element_type=jnp.float32
-        )
-        moved = part if moved is None else moved + part
+            moved = part if moved is None else moved + part
     return jnp.concatenate([fixed, moved.T], axis=1) if still else moved.T
 
 
-def add_pair(total_ref, latent, weight_ref, source, target):
-    total_ref[target] += product(latent, weight_ref, target * (target + 1) // 2 + source)
+def on_each_layer(layers, body):
+    for layer in range(layers):
+
+        @pl.when(lax.axis_index("layer") == layer)
+        def _():
+            body(layer)
 
 
 def decode_own_kernel(own_ref, weight_ref, total_ref):
-    layer, layers = lax.axis_index("layer"), total_ref.shape[0]
-    total_ref[...] = jnp.zeros_like(total_ref)
+    layers = total_ref.shape[0]
 
-    count = layers - layer
+    def body(layer):
+        for target in range(layers):
+            if layer <= target:
+                total_ref[target] = products([(layer, own_ref[...])], weight_ref, target)
+            else:
+                total_ref[target] = jnp.zeros(total_ref.shape[1:], total_ref.dtype)
 
-    @pl.when(count % 2 == 1)
-    def _():
-        add_pair(total_ref, own_ref[...], weight_ref, layer, layer)
-
-    for first in range(0, layers, 2):
-
-        @pl.when(first + 2 <= count)
-        def _():
-            for at in (first, first + 1):
-                add_pair(total_ref, own_ref[...], weight_ref, layer, layer + count % 2 + at)
+    on_each_layer(layers, body)
 
 
-def decode_far_kernel(parity, total_ref, far_ref, weight_ref, out_ref):
-    layer, layers = lax.axis_index("layer"), total_ref.shape[0]
-    out_ref[...] = total_ref[...]
-    source = layer ^ 2
-    count = jnp.where(layer % 2 == parity, layers - source, 0)
+def decode_more_kernel(offset, total_ref, latent_ref, weight_ref, out_ref):
+    layers = total_ref.shape[0]
 
-    @pl.when(count % 2 == 1)
-    def _():
-        add_pair(out_ref, far_ref[...], weight_ref, source, source)
+    def body(layer):
+        source = layer ^ offset
+        for target in range(layers):
+            total = total_ref[target]
+            if source <= target:
+                total = total + products([(source, latent_ref[...])], weight_ref, target)
+            out_ref[target] = total
 
-    for first in range(0, layers, 2):
-
-        @pl.when(first + 2 <= count)
-        def _():
-            for at in (first, first + 1):
-                add_pair(out_ref, far_ref[...], weight_ref, source, source + count % 2 + at)
+    on_each_layer(layers, body)
 
 
-def decode_last_kernel(total_ref, both_ref, weight_ref, out_ref, sum_ref):
-    layer, layers = lax.axis_index("layer"), total_ref.shape[0]
-    tokens = both_ref.shape[1]
-    sum_ref[...] = total_ref[...]
-    sources = (layer ^ 1, layer ^ 3)
-    first_count = layers - sources[0]
-    count = first_count + layers - sources[1]
+def decode_last_kernel(total_ref, last_ref, weight_ref, out_ref):
+    layers, tokens, _ = total_ref.shape
 
-    def step(at):
-        at_first = at < first_count
-        source = jnp.where(at_first, sources[0], sources[1])
-        target = jnp.where(at_first, sources[0] + at, sources[1] + at - first_count)
-        add_pair(sum_ref, both_ref[jnp.where(at_first, 0, 1)], weight_ref, source, target)
+    def body(layer):
+        source = layer ^ 3
+        for target in range(layers):
+            total = total_ref[target]
+            if source <= target:
+                total = total + products([(source, last_ref[...])], weight_ref, target)
+            for token in range(tokens):
+                out_ref[target * tokens + token] = total[token : token + 1, :]
 
-    for at in range(layers):
-        step(at)
-
-    @pl.when(count > layers)
-    def _():
-        for at in (layers, layers + 1):
-            step(at)
-
-    for target in range(layers):
-        total = sum_ref[target]
-        for token in range(tokens):
-            out_ref[target * tokens + token] = total[token : token + 1, :]
+    on_each_layer(layers, body)
 
 
 def finish_kernel(parts_ref, bias_ref, out_ref):
@@ -179,17 +163,15 @@
     weight = jnp.swapaxes(dec_weight, 1, 2)
     total = jax.ShapeDtypeStruct((layer_count, tokens, col_local), jnp.float32)
     far = swap(latent, layer_bit=2)
+    core = swap(latent, layer_bit=1)
     own_total = kernel(decode_own_kernel, total, "decode_own")(latent, weight)
-    odd_total = kernel(functools.partial(decode_far_kernel, 1), total, "decode_far_odd")(own_total, far, weight)
-    held, odd_total = lax.optimization_barrier((jnp.stack([latent, far]), odd_total))
-    both = swap(held, layer_bit=1)
-    even_total = kernel(functools.partial(decode_far_kernel, 0), total, "decode_far_even")(odd_total, far, weight)
+    chip_total = kernel(functools.partial(decode_more_kernel, 1), total, "decode_core")(own_total, core, weight)
+    far, chip_total = lax.optimization_barrier((far, chip_total))
+    last = swap(far, layer_bit=1)
+    far_total = kernel(functools.partial(decode_more_kernel, 2), total, "decode_far")(chip_total, far, weight)
     parts = kernel(
-        decode_last_kernel,
-        jax.ShapeDtypeStruct((layer_count * tokens, 1, col_local), jnp.float32),
-        "decode_last",
-        scratch_shapes=[pltpu.VMEM(total.shape, total.dtype)],
-    )(even_total, both, weight)
+        decode_last_kernel, jax.ShapeDtypeStruct((layer_count * tokens, 1, col_local), jnp.float32), "decode_last"
+    )(far_total, last, weight)
     arrived = lax.all_to_all(parts, AXES, 0, 0, tiled=True)
     return kernel(finish_kernel, jax.ShapeDtypeStruct((tok_local, 1, width), jnp.bfloat16), "finish")(
         arrived.reshape(layer_count, feat_count, tok_local, col_local), dec_bias

time: 35.1 us -> 34.5 us (0.983)
  blocking collectives: 24.5 us -> 23.9 us
  waiting for transfers between devices: 0.6 us -> 0.01 us
    ppermute x2 -> x3, waiting for transfers between devices: 0.6 us -> 0.01 us  [swap(): lax.ppermute(array, AXES, [(place(l, f), place(l ^ layer_bit, f ^ feat_bi...]
    all_to_all x1, blocking collectives: 10.2 us -> 9.67 us  [shards(): arrived = lax.all_to_all(parts, AXES, 0, 0, tiled=True)]
    ppermute x2 -> x3, starting transfers between devices: 1.65 us -> 1.99 us  [swap(): lax.ppermute(array, AXES, [(place(l, f), place(l ^ layer_bit, f ^ feat_bi...]
  transfers between devices with their start and end apart: 2 -> 3, of which waited for: 2 -> 0; matrix products, arithmetic and copies ran while one was open for 0% -> 0% of each run, Pallas kernels for 9% -> 13%
where the time goes in v4:
time: 34.5 us; the launch traced here: 34.3 us
  blocking collectives  23.9 us (69%)
  Pallas kernels  7.34 us (21%)
  starting transfers between devices  1.99 us (6%)
  local copies, waits for them, and re-layouts  0.9 us (3%)
    all_to_all x1, blocking collectives, shards(): gathered = lax.all_to_all(copies, 'feat', 0, 0, tiled=True)  14.3 us
    all_to_all x1, blocking collectives, shards(): arrived = lax.all_to_all(parts, AXES, 0, 0, tiled=True)  9.67 us
    pallas_call x7, Pallas kernels, call(): pl.pallas_call(body, out_shape=out_shape, in_specs=[VMEM] * len(operands)...  7.34 us
    ppermute x3, starting transfers between devices, swap(): lax.ppermute(array, AXES, [(place(l, f), place(l ^ layer_bit, f ^ feat_bi...  1.99 us
    unnamed x22, local copies, waits for them, and re-layouts  0.9 us
  transfers between devices with their start and end apart: 3, of which 0 were waited for; matrix products, arithmetic and copies ran while one was open for 0% of the time, Pallas kernels for 13%

profile of v4, /device:TPU:0, one launch (start us, length us, event | category | flops | bytes accessed | tf_op | source)
XLA Modules:
  0.0 34.3 jit_solution(13540963637983532606)
XLA Ops:
  0.0 0.0 copy-start
  0.0 0.0 copy-start.1
  0.0 0.8 %copy-done.1 = bf16[1,1,2304]{2,1,0:T(2,128)(2,1)S(1)} copy-done((bf16[1,1,2304]{2,1,0:T(2,128)(2,1)S(1)}, bf16[1,1,2304]{2,1,0:T(2,128)(2,1)}, u32[]{:S(2)}) %copy-start.1) | copy-done | bytes 4632
  0.9 0.0 copy-start.3
  0.9 0.0 copy-start.4
  0.9 0.0 slice-start
  0.9 0.0 slice-start.1
  0.9 0.0 slice-start.2
  0.9 0.0 slice-start.3
  0.9 14.3 %all_to_all.10.all_ref = f32[8,1,2304]{2,1,0:T(1,128)S(1)} all-to-all(f32[8,1,2304]{2,1,0:T(1,128)S(1)} %prepare.1), channel_id=1, replica_groups=mesh['layer'=4,'feat'=8] {'feat'}, dimensions={0} | all-to-all | bytes 147456 | tf_op jit(solution)/shard_map/all_to_all | solution.py:159
  15.2 0.0 copy-done
  15.2 0.0 copy-done.3
  15.2 0.0 copy-done.4
  15.2 0.0 slice-start.4
  15.2 0.0 slice-start.5
  15.2 1.5 %encode.1.own_ref = bf16[8,2048]{1,0:T(8,128)(2,1)S(1)} custom-call(f32[8,1,2304]{2,1,0:T(1,128)S(1)} %all_to_all.10.all_ref, bf16[2304,2048]{1,0:T(8,128)(2,1)S(1)} %bitcast.13, s32[16,18]{1,0:T(8,128)S(1)} %bitcast.14, f32[1,2048]{1,0:T(1,128)S(1)} %copy-done.4), custom_call_target="tpu_custom_call" | custom-call | flops 20000000000 | tf_op jit(solution)/shard_map/encode/pallas_call | solution.py:20
  16.7 0.1 collective-permute-start.1
  16.8 1.6 %collective-permute-start = (bf16[8,2048]{1,0:T(8,128)(2,1)S(1)}, bf16[8,2048]{1,0:T(8,128)(2,1)S(1)}, u32[]{:S(2)}, u32[]{:S(2)}) collective-permute-start(bf16[8,2048]{1,0:T(8,128)(2,1)S(1)} %encode.1.own_ref), channel_id=1, source_target_pairs={{0,16},{1,17},{2,18},{3,19},{4,20},{5,21},{6,22},{7,23},{8,24},{9,... | collective-permute-start | bytes 98312 | tf_op jit(solution)/shard_map/ppermute | solution.py:152
  18.3 0.0 slice-done
  18.3 0.0 slice-done.1
  18.4 0.0 slice-done.2
  18.4 0.0 slice-done.3
  18.4 0.0 slice-done.4
  18.4 0.0 slice-done.5
  18.4 1.8 %decode_own.1.total_ref = f32[4,8,576]{2,1,0:T(8,128)S(1)} custom-call(bf16[8,2048]{1,0:T(8,128)(2,1)S(1)} %encode.1.own_ref, bf16[10,576,2048]{2,1,0:T(8,128)(2,1)S(1)} %bitcast.9), custom_call_target="tpu_custom_call" | custom-call | flops 20000000000 | tf_op jit(solution)/shard_map/decode_own/pallas_call | solution.py:20
  20.2 0.0 collective-permute-done.1.latent_ref
  20.2 1.5 %decode_core.1.total_ref = f32[4,8,576]{2,1,0:T(8,128)S(1)} custom-call(f32[4,8,576]{2,1,0:T(8,128)S(1)} %decode_own.1.total_ref, bf16[8,2048]{1,0:T(8,128)(2,1)S(1)} %collective-permute-done.1.latent_ref, bf16[10,576,2048]{2,1,0:T(8,128)(2,1)S(1)} %bitcast.10), custom_call_target="tpu_custom_call" | custom-call | flops 20000000000 | tf_op jit(solution)/shard_map/decode_core/pallas_call | solution.py:20
  21.7 0.0 collective-permute-done.latent_ref
  21.7 0.3 collective-permute-start.2
  22.0 1.1 %decode_far.1.total_ref = f32[4,8,576]{2,1,0:T(8,128)S(1)} custom-call(f32[4,8,576]{2,1,0:T(8,128)S(1)} %decode_core.1.total_ref, bf16[8,2048]{1,0:T(8,128)(2,1)S(1)} %collective-permute-done.latent_ref, bf16[10,576,2048]{2,1,0:T(8,128)(2,1)S(1)} %bitcast.11), custom_call_target="tpu_custom_call" | custom-call | flops 20000000000 | tf_op jit(solution)/shard_map/decode_far/pallas_call | solution.py:20
  23.1 0.0 copy-start.2
  23.2 0.0 collective-permute-done.2.last_ref
  23.2 0.7 %decode_last.1 = f32[32,1,576]{2,1,0:T(1,128)S(1)} custom-call(f32[4,8,576]{2,1,0:T(8,128)S(1)} %decode_far.1.total_ref, bf16[8,2048]{1,0:T(8,128)(2,1)S(1)} %collective-permute-done.2.last_ref, bf16[10,576,2048]{2,1,0:T(8,128)(2,1)S(1)} %bitcast.12), custom_call_target="tpu_custom_call" | custom-call | flops 20000000000 | tf_op jit(solution)/shard_map/decode_last/pallas_call | solution.py:20
  23.9 9.7 %all_to_all.11 = f32[32,1,576]{2,1,0:T(1,128)S(1)} all-to-all(f32[32,1,576]{2,1,0:T(1,128)S(1)} %decode_last.1), channel_id=1, replica_groups=mesh['layer'=4,'feat'=8] {'layer','feat'}, dimensions={0} | all-to-all | bytes 147456 | tf_op jit(solution)/shard_map/all_to_all | solution.py:175
  33.5 0.0 copy-done.2
  33.5 0.7 %finish.1 = bf16[1,1,2304]{2,1,0:T(2,128)(2,1)} custom-call(f32[4,8,1,576]{3,2,1,0:T(1,128)S(1)} %bitcast.6, f32[1,2304]{1,0:T(1,128)S(1)} %copy-done.2), custom_call_target="tpu_custom_call" | custom-call | flops 20000000000 | tf_op jit(solution)/shard_map/finish/pallas_call | solution.py:20
  (2 shorter events, 0.0 us)
Async XLA Ops:
  0.0 15.2 %copy-start = (bf16[1,2304,2048]{2,1,0:T(8,128)(2,1)S(1)}, bf16[1,2304,2048]{2,1,0:T(8,128)(2,1)}, u32[]{:S(2)}) copy-start(bf16[1,2304,2048]{2,1,0:T(8,128)(2,1)} %param.7) | copy-start | bytes 28311556
  0.0 0.8 %copy-start.1 = (bf16[1,1,2304]{2,1,0:T(2,128)(2,1)S(1)}, bf16[1,1,2304]{2,1,0:T(2,128)(2,1)}, u32[]{:S(2)}) copy-start(bf16[1,1,2304]{2,1,0:T(2,128)(2,1)} %own_ref.1) | copy-start | bytes 13828
  0.9 14.3 %copy-start.3 = (s32[1,18,16]{1,2,0:T(8,128)S(1)}, s32[1,18,16]{1,2,0:T(8,128)}, u32[]{:S(2)}) copy-start(s32[1,18,16]{1,2,0:T(8,128)} %param.8) | copy-start | bytes 3460
  0.9 14.3 %copy-start.4 = (f32[1,2048]{1,0:T(1,128)S(1)}, f32[1,2048]{1,0:T(1,128)}, u32[]{:S(2)}) copy-start(f32[1,2048]{1,0:T(1,128)} %bias_ref.2) | copy-start | bytes 24580
  0.9 17.5 %slice-start = ((s8[23592960]{0:T(1024)(128)(4,1)}), s8[4194304]{0:T(1024)(128)(4,1)S(1)}, s32[]{:S(2)}) async-start(s8[23592960]{0:T(1024)(128)(4,1)} %bitcast.7), calls=%async_computation.2 | async-start | bytes 8388608
  0.9 17.5 %slice-start.1 = ((s8[23592960]{0:T(1024)(128)(4,1)}), s8[4194304]{0:T(1024)(128)(4,1)S(1)}, s32[]{:S(2)}) async-start(s8[23592960]{0:T(1024)(128)(4,1)} %bitcast.7), calls=%async_computation.3 | async-start | bytes 8388608
  0.9 17.5 %slice-start.2 = ((s8[23592960]{0:T(1024)(128)(4,1)}), s8[4194304]{0:T(1024)(128)(4,1)S(1)}, s32[]{:S(2)}) async-start(s8[23592960]{0:T(1024)(128)(4,1)} %bitcast.7), calls=%async_computation.4 | async-start | bytes 8388608
  0.9 17.5 %slice-start.3 = ((s8[23592960]{0:T(1024)(128)(4,1)}), s8[4194304]{0:T(1024)(128)(4,1)S(1)}, s32[]{:S(2)}) async-start(s8[23592960]{0:T(1024)(128)(4,1)} %bitcast.7), calls=%async_computation.5 | async-start | bytes 8388608
  15.2 3.2 %slice-start.4 = ((s8[23592960]{0:T(1024)(128)(4,1)}), s8[4194304]{0:T(1024)(128)(4,1)S(1)}, s32[]{:S(2)}) async-start(s8[23592960]{0:T(1024)(128)(4,1)} %bitcast.7), calls=%async_computation.6 | async-start | bytes 8388608
  15.2 3.2 %slice-start.5 = ((s8[23592960]{0:T(1024)(128)(4,1)}), s8[2621440]{0:T(1024)(128)(4,1)S(1)}, s32[]{:S(2)}) async-start(s8[23592960]{0:T(1024)(128)(4,1)} %bitcast.7), calls=%async_computation.7 | async-start | bytes 5242880
  16.7 3.5 %collective-permute-start.1 = (bf16[8,2048]{1,0:T(8,128)(2,1)S(1)}, bf16[8,2048]{1,0:T(8,128)(2,1)S(1)}, u32[]{:S(2)}, u32[]{:S(2)}) collective-permute-start(bf16[8,2048]{1,0:T(8,128)(2,1)S(1)} %encode.1.own_ref), channel_id=1, source_target_pairs={{0,8},{1,9},{2,10},{3,11},{4,12},{5,13},{6,14},{7,15},{8,0},{9,1},... | collective-permute-start | bytes 98312 | tf_op jit(solution)/shard_map/ppermute | solution.py:152
  16.8 4.9 %collective-permute-start = (bf16[8,2048]{1,0:T(8,128)(2,1)S(1)}, bf16[8,2048]{1,0:T(8,128)(2,1)S(1)}, u32[]{:S(2)}, u32[]{:S(2)}) collective-permute-start(bf16[8,2048]{1,0:T(8,128)(2,1)S(1)} %encode.1.own_ref), channel_id=1, source_target_pairs={{0,16},{1,17},{2,18},{3,19},{4,20},{5,21},{6,22},{7,23},{8,24},{9,... | collective-permute-start | bytes 98312 | tf_op jit(solution)/shard_map/ppermute | solution.py:152
  21.7 1.5 %collective-permute-start.2 = (bf16[8,2048]{1,0:T(8,128)(2,1)S(1)}, bf16[8,2048]{1,0:T(8,128)(2,1)S(1)}, u32[]{:S(2)}, u32[]{:S(2)}) collective-permute-start(bf16[8,2048]{1,0:T(8,128)(2,1)S(1)} %collective-permute-done.latent_ref), channel_id=1, source_target_pairs={{0,8},{1,9},{2,10},{3,11},{4,12},{5,13},{6,14},{7,15},{8,0},{9,1},... | collective-permute-start | bytes 98312 | tf_op jit(solution)/shard_map/ppermute | solution.py:152
  23.1 10.4 %copy-start.2 = (f32[1,2304]{1,0:T(1,128)S(1)}, f32[1,2304]{1,0:T(1,128)}, u32[]{:S(2)}) copy-start(f32[1,2304]{1,0:T(1,128)} %bias_ref.3) | copy-start | bytes 27652

commit v5 on v4

--- a/solution.py
+++ b/solution.py
@@ -11,11 +11,11 @@
 AXES = ("layer", "feat")
 VMEM = pl.BlockSpec(memory_space=pltpu.VMEM)
 LIMIT = 8 * 1024 * 1024
-WORK = 20_000_000_000
+WORK = 2_000_000_000
 OVER_ROWS = (((1,), (1,)), ((), ()))
 
 
-def kernel(body, out_shape, name, scratch_shapes=()):
+def kernel(body, out_shape, name, scratch_shapes=(), work=WORK):
     def call(*operands):
         return pl.pallas_call(
             body,
@@ -24,7 +24,7 @@
             out_specs=VMEM,
             scratch_shapes=scratch_shapes,
             compiler_params=pltpu.CompilerParams(vmem_limit_bytes=LIMIT),
-            cost_estimate=pl.CostEstimate(flops=WORK, bytes_accessed=0, transcendentals=0),
+            cost_estimate=pl.CostEstimate(flops=work, bytes_accessed=0, transcendentals=0),
             name=name,
         )(*operands)
 
@@ -115,7 +115,7 @@
     layers, tokens, _ = total_ref.shape
 
     def body(layer):
-        source = layer ^ 3
+        source = layer ^ 2
         for target in range(layers):
             total = total_ref[target]
             if source <= target:
@@ -155,20 +155,20 @@
             [(place(l, f), place(l ^ layer_bit, f ^ feat_bit)) for l, f in everywhere if l % 2 in parities],
         )
 
-    copies = kernel(prepare_kernel, jax.ShapeDtypeStruct((tokens, 1, width), jnp.float32), "prepare")(resid_stream)
+    copies = kernel(prepare_kernel, jax.ShapeDtypeStruct((tokens, 1, width), jnp.float32), "prepare", work=20 * WORK)(resid_stream)
     gathered = lax.all_to_all(copies, "feat", 0, 0, tiled=True)
     latent = kernel(encode_kernel, jax.ShapeDtypeStruct((tokens, feat_local), jnp.bfloat16), "encode")(
         gathered, enc_mantissa[0], jnp.swapaxes(enc_exponent[0], 0, 1), enc_bias
     )
     weight = jnp.swapaxes(dec_weight, 1, 2)
     total = jax.ShapeDtypeStruct((layer_count, tokens, col_local), jnp.float32)
-    far = swap(latent, layer_bit=2)
+    far = swap(latent, layer_bit=3)
     core = swap(latent, layer_bit=1)
     own_total = kernel(decode_own_kernel, total, "decode_own")(latent, weight)
     chip_total = kernel(functools.partial(decode_more_kernel, 1), total, "decode_core")(own_total, core, weight)
     far, chip_total = lax.optimization_barrier((far, chip_total))
     last = swap(far, layer_bit=1)
-    far_total = kernel(functools.partial(decode_more_kernel, 2), total, "decode_far")(chip_total, far, weight)
+    far_total = kernel(functools.partial(decode_more_kernel, 3), total, "decode_far")(chip_total, far, weight)
     parts = kernel(
         decode_last_kernel, jax.ShapeDtypeStruct((layer_count * tokens, 1, col_local), jnp.float32), "decode_last"
     )(far_total, last, weight)

time: 34.5 us -> 34.4 us (level)
    unnamed x22 -> x12, local copies, waits for them, and re-layouts: 0.9 us -> 0.87 us
  transfers between devices with their start and end apart: 3 -> 3, of which waited for: 0 -> 1; matrix products, arithmetic and copies ran while one was open for 0% -> 0% of each run, Pallas kernels for 13% -> 12%
where the time goes in v5:
time: 34.4 us; the launch traced here: 34.1 us
  blocking collectives  23.8 us (69%)
  Pallas kernels  7.26 us (21%)
  starting transfers between devices  1.95 us (6%)
  local copies, waits for them, and re-layouts  0.87 us (3%)
    all_to_all x1, blocking collectives, shards(): gathered = lax.all_to_all(copies, 'feat', 0, 0, tiled=True)  14.3 us
    all_to_all x1, blocking collectives, shards(): arrived = lax.all_to_all(parts, AXES, 0, 0, tiled=True)  9.54 us
    pallas_call x7, Pallas kernels, call(): pl.pallas_call(body, out_shape=out_shape, in_specs=[VMEM] * len(operands)...  7.26 us
    ppermute x3, starting transfers between devices, swap(): lax.ppermute(array, AXES, [(place(l, f), place(l ^ layer_bit, f ^ feat_bi...  1.95 us
    unnamed x12, local copies, waits for them, and re-layouts  0.87 us
  transfers between devices with their start and end apart: 3, of which 1 were waited for; matrix products, arithmetic and copies ran while one was open for 0% of the time, Pallas kernels for 12%

profile of v5, /device:TPU:0, one launch (start us, length us, event | category | flops | bytes accessed | tf_op | source)
XLA Modules:
  0.0 34.1 jit_solution(17455502345183283971)
XLA Ops:
  0.0 0.0 copy-start.3
  0.0 0.0 copy-start.2
  0.0 0.0 copy-start.1
  0.0 0.0 copy-start.4
  0.0 0.8 %copy-done.4 = bf16[1,1,2304]{2,1,0:T(2,128)(2,1)S(1)} copy-done((bf16[1,1,2304]{2,1,0:T(2,128)(2,1)S(1)}, bf16[1,1,2304]{2,1,0:T(2,128)(2,1)}, u32[]{:S(2)}) %copy-start.4) | copy-done | bytes 4632
  0.9 0.0 copy-start
  0.9 14.3 %all_to_all.10.all_ref = f32[8,1,2304]{2,1,0:T(1,128)S(1)} all-to-all(f32[8,1,2304]{2,1,0:T(1,128)S(1)} %prepare.1), channel_id=1, replica_groups=mesh['layer'=4,'feat'=8] {'feat'}, dimensions={0} | all-to-all | bytes 147456 | tf_op jit(solution)/shard_map/all_to_all | solution.py:159
  15.2 0.0 copy-done.3
  15.2 0.0 copy-done.2
  15.2 0.0 copy-done.1
  15.2 1.4 %encode.1.own_ref = bf16[8,2048]{1,0:T(8,128)(2,1)S(1)} custom-call(f32[8,1,2304]{2,1,0:T(1,128)S(1)} %all_to_all.10.all_ref, bf16[2304,2048]{1,0:T(8,128)(2,1)S(1)} %bitcast.10, s32[16,18]{1,0:T(8,128)S(1)} %bitcast.12, f32[1,2048]{1,0:T(1,128)S(1)} %copy-done.3), custom_call_target="tpu_custom_call" | custom-call | flops 2000000000 | tf_op jit(solution)/shard_map/encode/pallas_call | solution.py:20
  16.6 0.1 collective-permute-start.1
  16.7 1.6 %collective-permute-start = (bf16[8,2048]{1,0:T(8,128)(2,1)S(1)}, bf16[8,2048]{1,0:T(8,128)(2,1)S(1)}, u32[]{:S(2)}, u32[]{:S(2)}) collective-permute-start(bf16[8,2048]{1,0:T(8,128)(2,1)S(1)} %encode.1.own_ref), channel_id=1, source_target_pairs={{0,24},{1,25},{2,26},{3,27},{4,28},{5,29},{6,30},{7,31},{8,16},{9,... | collective-permute-start | bytes 98312 | tf_op jit(solution)/shard_map/ppermute | solution.py:152
  18.3 0.0 copy-done
  18.3 1.8 %decode_own.1.total_ref = f32[4,8,576]{2,1,0:T(8,128)S(1)} custom-call(bf16[8,2048]{1,0:T(8,128)(2,1)S(1)} %encode.1.own_ref, bf16[10,576,2048]{2,1,0:T(8,128)(2,1)S(1)} %bitcast.6), custom_call_target="tpu_custom_call" | custom-call | flops 2000000000 | tf_op jit(solution)/shard_map/decode_own/pallas_call | solution.py:20
  20.1 0.0 collective-permute-done.1.latent_ref
  20.1 1.5 %decode_core.1.total_ref = f32[4,8,576]{2,1,0:T(8,128)S(1)} custom-call(f32[4,8,576]{2,1,0:T(8,128)S(1)} %decode_own.1.total_ref, bf16[8,2048]{1,0:T(8,128)(2,1)S(1)} %collective-permute-done.1.latent_ref, bf16[10,576,2048]{2,1,0:T(8,128)(2,1)S(1)} %bitcast.7), custom_call_target="tpu_custom_call" | custom-call | flops 2000000000 | tf_op jit(solution)/shard_map/decode_core/pallas_call | solution.py:20
  21.6 0.0 copy-start.5
  21.6 0.0 collective-permute-done.latent_ref
  21.6 0.2 collective-permute-start.2
  21.8 0.8 %decode_far.1.total_ref = f32[4,8,576]{2,1,0:T(8,128)S(1)} custom-call(f32[4,8,576]{2,1,0:T(8,128)S(1)} %decode_core.1.total_ref, bf16[8,2048]{1,0:T(8,128)(2,1)S(1)} %collective-permute-done.latent_ref, bf16[10,576,2048]{2,1,0:T(8,128)(2,1)S(1)} %bitcast.8), custom_call_target="tpu_custom_call" | custom-call | flops 2000000000 | tf_op jit(solution)/shard_map/decode_far/pallas_call | solution.py:20
  22.7 0.2 collective-permute-done.2.last_ref
  22.9 1.0 %decode_last.1 = f32[32,1,576]{2,1,0:T(1,128)S(1)} custom-call(f32[4,8,576]{2,1,0:T(8,128)S(1)} %decode_far.1.total_ref, bf16[8,2048]{1,0:T(8,128)(2,1)S(1)} %collective-permute-done.2.last_ref, bf16[10,576,2048]{2,1,0:T(8,128)(2,1)S(1)} %bitcast.9), custom_call_target="tpu_custom_call" | custom-call | flops 2000000000 | tf_op jit(solution)/shard_map/decode_last/pallas_call | solution.py:20
  23.8 9.5 %all_to_all.11 = f32[32,1,576]{2,1,0:T(1,128)S(1)} all-to-all(f32[32,1,576]{2,1,0:T(1,128)S(1)} %decode_last.1), channel_id=1, replica_groups=mesh['layer'=4,'feat'=8] {'layer','feat'}, dimensions={0} | all-to-all | bytes 147456 | tf_op jit(solution)/shard_map/all_to_all | solution.py:175
  33.4 0.0 copy-done.5
  33.4 0.7 %finish.1 = bf16[1,1,2304]{2,1,0:T(2,128)(2,1)} custom-call(f32[4,8,1,576]{3,2,1,0:T(1,128)S(1)} %bitcast.11, f32[1,2304]{1,0:T(1,128)S(1)} %copy-done.5), custom_call_target="tpu_custom_call" | custom-call | flops 2000000000 | tf_op jit(solution)/shard_map/finish/pallas_call | solution.py:20
  (1 shorter events, 0.0 us)
Async XLA Ops:
  0.0 15.2 %copy-start.3 = (f32[1,2048]{1,0:T(1,128)S(1)}, f32[1,2048]{1,0:T(1,128)}, u32[]{:S(2)}) copy-start(f32[1,2048]{1,0:T(1,128)} %bias_ref.2) | copy-start | bytes 24580
  0.0 15.2 %copy-start.2 = (s32[1,18,16]{1,2,0:T(8,128)S(1)}, s32[1,18,16]{1,2,0:T(8,128)}, u32[]{:S(2)}) copy-start(s32[1,18,16]{1,2,0:T(8,128)} %param.8) | copy-start | bytes 3460
  0.0 15.2 %copy-start.1 = (bf16[1,2304,2048]{2,1,0:T(8,128)(2,1)S(1)}, bf16[1,2304,2048]{2,1,0:T(8,128)(2,1)}, u32[]{:S(2)}) copy-start(bf16[1,2304,2048]{2,1,0:T(8,128)(2,1)} %param.7) | copy-start | bytes 28311556
  0.0 0.8 %copy-start.4 = (bf16[1,1,2304]{2,1,0:T(2,128)(2,1)S(1)}, bf16[1,1,2304]{2,1,0:T(2,128)(2,1)}, u32[]{:S(2)}) copy-start(bf16[1,1,2304]{2,1,0:T(2,128)(2,1)} %own_ref.1) | copy-start | bytes 13828
  0.9 17.5 %copy-start = (bf16[10,2048,576]{1,2,0:T(8,128)(2,1)S(1)}, bf16[10,2048,576]{1,2,0:T(8,128)(2,1)}, u32[]{:S(2)}) copy-start(bf16[10,2048,576]{1,2,0:T(8,128)(2,1)} %param.10) | copy-start | bytes 70778880
  16.6 3.5 %collective-permute-start.1 = (bf16[8,2048]{1,0:T(8,128)(2,1)S(1)}, bf16[8,2048]{1,0:T(8,128)(2,1)S(1)}, u32[]{:S(2)}, u32[]{:S(2)}) collective-permute-start(bf16[8,2048]{1,0:T(8,128)(2,1)S(1)} %encode.1.own_ref), channel_id=1, source_target_pairs={{0,8},{1,9},{2,10},{3,11},{4,12},{5,13},{6,14},{7,15},{8,0},{9,1},... | collective-permute-start | bytes 98312 | tf_op jit(solution)/shard_map/ppermute | solution.py:152
  16.7 4.9 %collective-permute-start = (bf16[8,2048]{1,0:T(8,128)(2,1)S(1)}, bf16[8,2048]{1,0:T(8,128)(2,1)S(1)}, u32[]{:S(2)}, u32[]{:S(2)}) collective-permute-start(bf16[8,2048]{1,0:T(8,128)(2,1)S(1)} %encode.1.own_ref), channel_id=1, source_target_pairs={{0,24},{1,25},{2,26},{3,27},{4,28},{5,29},{6,30},{7,31},{8,16},{9,... | collective-permute-start | bytes 98312 | tf_op jit(solution)/shard_map/ppermute | solution.py:152
  21.6 11.8 %copy-start.5 = (f32[1,2304]{1,0:T(1,128)S(1)}, f32[1,2304]{1,0:T(1,128)}, u32[]{:S(2)}) copy-start(f32[1,2304]{1,0:T(1,128)} %bias_ref.3) | copy-start | bytes 27652
  21.6 1.3 %collective-permute-start.2 = (bf16[8,2048]{1,0:T(8,128)(2,1)S(1)}, bf16[8,2048]{1,0:T(8,128)(2,1)S(1)}, u32[]{:S(2)}, u32[]{:S(2)}) collective-permute-start(bf16[8,2048]{1,0:T(8,128)(2,1)S(1)} %collective-permute-done.latent_ref), channel_id=1, source_target_pairs={{0,8},{1,9},{2,10},{3,11},{4,12},{5,13},{6,14},{7,15},{8,0},{9,1},... | collective-permute-start | bytes 98312 | tf_op jit(solution)/shard_map/ppermute | solution.py:152

commit v6 on v5

--- a/solution.py
+++ b/solution.py
@@ -84,13 +84,15 @@
             body(layer)
 
 
-def decode_own_kernel(own_ref, weight_ref, total_ref):
+def decode_chip_kernel(own_ref, core_ref, weight_ref, total_ref):
     layers = total_ref.shape[0]
 
     def body(layer):
+        latents = [(layer, own_ref[...]), (layer ^ 1, core_ref[...])]
         for target in range(layers):
-            if layer <= target:
-                total_ref[target] = products([(layer, own_ref[...])], weight_ref, target)
+            reached = [entry for entry in latents if entry[0] <= target]
+            if reached:
+                total_ref[target] = products(reached, weight_ref, target)
             else:
                 total_ref[target] = jnp.zeros(total_ref.shape[1:], total_ref.dtype)
 
@@ -162,16 +164,15 @@
     )
     weight = jnp.swapaxes(dec_weight, 1, 2)
     total = jax.ShapeDtypeStruct((layer_count, tokens, col_local), jnp.float32)
-    far = swap(latent, layer_bit=3)
     core = swap(latent, layer_bit=1)
-    own_total = kernel(decode_own_kernel, total, "decode_own")(latent, weight)
-    chip_total = kernel(functools.partial(decode_more_kernel, 1), total, "decode_core")(own_total, core, weight)
-    far, chip_total = lax.optimization_barrier((far, chip_total))
-    last = swap(far, layer_bit=1)
-    far_total = kernel(functools.partial(decode_more_kernel, 3), total, "decode_far")(chip_total, far, weight)
+    other = swap(latent, layer_bit=3)
+    held, core = lax.optimization_barrier((latent, core))
+    same = swap(held, layer_bit=2)
+    chip_total = kernel(decode_chip_kernel, total, "decode_chip")(latent, core, weight)
+    most_total = kernel(functools.partial(decode_more_kernel, 3), total, "decode_other")(chip_total, other, weight)
     parts = kernel(
-        decode_last_kernel, jax.ShapeDtypeStruct((layer_count * tokens, 1, col_local), jnp.float32), "decode_last"
-    )(far_total, last, weight)
+        decode_last_kernel, jax.ShapeDtypeStruct((layer_count * tokens, 1, col_local), jnp.float32), "decode_same"
+    )(most_total, same, weight)
     arrived = lax.all_to_all(parts, AXES, 0, 0, tiled=True)
     return kernel(finish_kernel, jax.ShapeDtypeStruct((tok_local, 1, width), jnp.bfloat16), "finish")(
         arrived.reshape(layer_count, feat_count, tok_local, col_local), dec_bias

time: 34.4 us -> 34.2 us (level)
  starting transfers between devices: 1.95 us -> 2.78 us
  Pallas kernels: 7.26 us -> 6.81 us
  blocking collectives: 23.8 us -> 23.4 us
    ppermute x3, starting transfers between devices: 1.95 us -> 2.78 us  [swap(): lax.ppermute(array, AXES, [(place(l, f), place(l ^ layer_bit, f ^ feat_bi...]
    pallas_call x7 -> x6, Pallas kernels: 7.26 us -> 6.81 us  [call(): pl.pallas_call(body, out_shape=out_shape, in_specs=[VMEM] * len(operands)...]
    all_to_all x1, blocking collectives: 9.54 us -> 9.12 us  [shards(): arrived = lax.all_to_all(parts, AXES, 0, 0, tiled=True)]
  transfers between devices with their start and end apart: 3 -> 3, of which waited for: 1 -> 0; matrix products, arithmetic and copies ran while one was open for 0% -> 0% of each run, Pallas kernels for 12% -> 10%
where the time goes in v6:
time: 34.2 us; the launch traced here: 33.9 us
  blocking collectives  23.4 us (68%)
  Pallas kernels  6.81 us (20%)
  starting transfers between devices  2.78 us (8%)
  local copies, waits for them, and re-layouts  0.87 us (3%)
    all_to_all x1, blocking collectives, shards(): gathered = lax.all_to_all(copies, 'feat', 0, 0, tiled=True)  14.3 us
    all_to_all x1, blocking collectives, shards(): arrived = lax.all_to_all(parts, AXES, 0, 0, tiled=True)  9.12 us
    pallas_call x6, Pallas kernels, call(): pl.pallas_call(body, out_shape=out_shape, in_specs=[VMEM] * len(operands)...  6.81 us
    ppermute x3, starting transfers between devices, swap(): lax.ppermute(array, AXES, [(place(l, f), place(l ^ layer_bit, f ^ feat_bi...  2.78 us
    unnamed x12, local copies, waits for them, and re-layouts  0.87 us
  transfers between devices with their start and end apart: 3, of which 0 were waited for; matrix products, arithmetic and copies ran while one was open for 0% of the time, Pallas kernels for 10%

profile of v6, /device:TPU:0, one launch (start us, length us, event | category | flops | bytes accessed | tf_op | source)
XLA Modules:
  0.0 33.9 jit_solution(9627078151852659570)
XLA Ops:
  0.0 0.0 copy-start.3
  0.0 0.0 copy-start.2
  0.0 0.0 copy-start.1
  0.0 0.0 copy-start.4
  0.0 0.8 %copy-done.4 = bf16[1,1,2304]{2,1,0:T(2,128)(2,1)S(1)} copy-done((bf16[1,1,2304]{2,1,0:T(2,128)(2,1)S(1)}, bf16[1,1,2304]{2,1,0:T(2,128)(2,1)}, u32[]{:S(2)}) %copy-start.4) | copy-done | bytes 4632
  0.9 0.0 copy-start
  0.9 14.3 %all_to_all.10.all_ref = f32[8,1,2304]{2,1,0:T(1,128)S(1)} all-to-all(f32[8,1,2304]{2,1,0:T(1,128)S(1)} %prepare.1), channel_id=1, replica_groups=mesh['layer'=4,'feat'=8] {'feat'}, dimensions={0} | all-to-all | bytes 147456 | tf_op jit(solution)/shard_map/all_to_all | solution.py:161
  15.2 0.0 copy-done.3
  15.2 0.0 copy-done.2
  15.2 0.0 copy-done.1
  15.2 1.4 %encode.1.own_ref = bf16[8,2048]{1,0:T(8,128)(2,1)S(1)} custom-call(f32[8,1,2304]{2,1,0:T(1,128)S(1)} %all_to_all.10.all_ref, bf16[2304,2048]{1,0:T(8,128)(2,1)S(1)} %bitcast.9, s32[16,18]{1,0:T(8,128)S(1)} %bitcast.11, f32[1,2048]{1,0:T(1,128)S(1)} %copy-done.3), custom_call_target="tpu_custom_call" | custom-call | flops 2000000000 | tf_op jit(solution)/shard_map/encode/pallas_call | solution.py:20
  16.6 0.1 collective-permute-start
  16.7 1.6 %collective-permute-start.1 = (bf16[8,2048]{1,0:T(8,128)(2,1)S(1)}, bf16[8,2048]{1,0:T(8,128)(2,1)S(1)}, u32[]{:S(2)}, u32[]{:S(2)}) collective-permute-start(bf16[8,2048]{1,0:T(8,128)(2,1)S(1)} %encode.1.own_ref), channel_id=1, source_target_pairs={{0,24},{1,25},{2,26},{3,27},{4,28},{5,29},{6,30},{7,31},{8,16},{9,... | collective-permute-start | bytes 98312 | tf_op jit(solution)/shard_map/ppermute | solution.py:154
  18.3 0.0 collective-permute-done.core_ref
  18.3 1.1 %collective-permute-start.2 = (bf16[8,2048]{1,0:T(8,128)(2,1)S(1)}, bf16[8,2048]{1,0:T(8,128)(2,1)S(1)}, u32[]{:S(2)}, u32[]{:S(2)}) collective-permute-start(bf16[8,2048]{1,0:T(8,128)(2,1)S(1)} %encode.1.own_ref), channel_id=1, source_target_pairs={{0,16},{1,17},{2,18},{3,19},{4,20},{5,21},{6,22},{7,23},{8,24},{9,... | collective-permute-start | bytes 98312 | tf_op jit(solution)/shard_map/ppermute | solution.py:154
  19.4 0.0 copy-done
  19.4 2.8 %decode_chip.1.total_ref = f32[4,8,576]{2,1,0:T(8,128)S(1)} custom-call(bf16[8,2048]{1,0:T(8,128)(2,1)S(1)} %encode.1.own_ref, bf16[8,2048]{1,0:T(8,128)(2,1)S(1)} %collective-permute-done.core_ref, bf16[10,576,2048]{2,1,0:T(8,128)(2,1)S(1)} %bitcast.6), custom_call_target="tpu_custom_call" | custom-call | flops 2000000000 | tf_op jit(solution)/shard_map/decode_chip/pallas_call | solution.py:20
  22.2 0.0 copy-start.5
  22.2 0.0 collective-permute-done.1.latent_ref
  22.2 0.7 %decode_other.1.total_ref = f32[4,8,576]{2,1,0:T(8,128)S(1)} custom-call(f32[4,8,576]{2,1,0:T(8,128)S(1)} %decode_chip.1.total_ref, bf16[8,2048]{1,0:T(8,128)(2,1)S(1)} %collective-permute-done.1.latent_ref, bf16[10,576,2048]{2,1,0:T(8,128)(2,1)S(1)} %bitcast.7), custom_call_target="tpu_custom_call" | custom-call | flops 2000000000 | tf_op jit(solution)/shard_map/decode_other/pallas_call | solution.py:20
  22.9 0.0 collective-permute-done.2.last_ref
  22.9 1.1 %decode_same.1 = f32[32,1,576]{2,1,0:T(1,128)S(1)} custom-call(f32[4,8,576]{2,1,0:T(8,128)S(1)} %decode_other.1.total_ref, bf16[8,2048]{1,0:T(8,128)(2,1)S(1)} %collective-permute-done.2.last_ref, bf16[10,576,2048]{2,1,0:T(8,128)(2,1)S(1)} %bitcast.8), custom_call_target="tpu_custom_call" | custom-call | flops 2000000000 | tf_op jit(solution)/shard_map/decode_same/pallas_call | solution.py:20
  24.0 9.1 %all_to_all.11 = f32[32,1,576]{2,1,0:T(1,128)S(1)} all-to-all(f32[32,1,576]{2,1,0:T(1,128)S(1)} %decode_same.1), channel_id=1, replica_groups=mesh['layer'=4,'feat'=8] {'layer','feat'}, dimensions={0} | all-to-all | bytes 147456 | tf_op jit(solution)/shard_map/all_to_all | solution.py:176
  33.1 0.0 copy-done.5
  33.1 0.7 %finish.1 = bf16[1,1,2304]{2,1,0:T(2,128)(2,1)} custom-call(f32[4,8,1,576]{3,2,1,0:T(1,128)S(1)} %bitcast.10, f32[1,2304]{1,0:T(1,128)S(1)} %copy-done.5), custom_call_target="tpu_custom_call" | custom-call | flops 2000000000 | tf_op jit(solution)/shard_map/finish/pallas_call | solution.py:20
  (1 shorter events, 0.0 us)
Async XLA Ops:
  0.0 15.2 %copy-start.3 = (f32[1,2048]{1,0:T(1,128)S(1)}, f32[1,2048]{1,0:T(1,128)}, u32[]{:S(2)}) copy-start(f32[1,2048]{1,0:T(1,128)} %bias_ref.2) | copy-start | bytes 24580
  0.0 15.2 %copy-start.2 = (s32[1,18,16]{1,2,0:T(8,128)S(1)}, s32[1,18,16]{1,2,0:T(8,128)}, u32[]{:S(2)}) copy-start(s32[1,18,16]{1,2,0:T(8,128)} %param.8) | copy-start | bytes 3460
  0.0 15.2 %copy-start.1 = (bf16[1,2304,2048]{2,1,0:T(8,128)(2,1)S(1)}, bf16[1,2304,2048]{2,1,0:T(8,128)(2,1)}, u32[]{:S(2)}) copy-start(bf16[1,2304,2048]{2,1,0:T(8,128)(2,1)} %param.7) | copy-start | bytes 28311556
  0.0 0.8 %copy-start.4 = (bf16[1,1,2304]{2,1,0:T(2,128)(2,1)S(1)}, bf16[1,1,2304]{2,1,0:T(2,128)(2,1)}, u32[]{:S(2)}) copy-start(bf16[1,1,2304]{2,1,0:T(2,128)(2,1)} %own_ref.1) | copy-start | bytes 13828
  0.9 18.5 %copy-start = (bf16[10,2048,576]{1,2,0:T(8,128)(2,1)S(1)}, bf16[10,2048,576]{1,2,0:T(8,128)(2,1)}, u32[]{:S(2)}) copy-start(bf16[10,2048,576]{1,2,0:T(8,128)(2,1)} %param.10) | copy-start | bytes 70778880
  16.6 1.7 %collective-permute-start = (bf16[8,2048]{1,0:T(8,128)(2,1)S(1)}, bf16[8,2048]{1,0:T(8,128)(2,1)S(1)}, u32[]{:S(2)}, u32[]{:S(2)}) collective-permute-start(bf16[8,2048]{1,0:T(8,128)(2,1)S(1)} %encode.1.own_ref), channel_id=1, source_target_pairs={{0,8},{1,9},{2,10},{3,11},{4,12},{5,13},{6,14},{7,15},{8,0},{9,1},... | collective-permute-start | bytes 98312 | tf_op jit(solution)/shard_map/ppermute | solution.py:154
  16.7 5.5 %collective-permute-start.1 = (bf16[8,2048]{1,0:T(8,128)(2,1)S(1)}, bf16[8,2048]{1,0:T(8,128)(2,1)S(1)}, u32[]{:S(2)}, u32[]{:S(2)}) collective-permute-start(bf16[8,2048]{1,0:T(8,128)(2,1)S(1)} %encode.1.own_ref), channel_id=1, source_target_pairs={{0,24},{1,25},{2,26},{3,27},{4,28},{5,29},{6,30},{7,31},{8,16},{9,... | collective-permute-start | bytes 98312 | tf_op jit(solution)/shard_map/ppermute | solution.py:154
  18.3 4.6 %collective-permute-start.2 = (bf16[8,2048]{1,0:T(8,128)(2,1)S(1)}, bf16[8,2048]{1,0:T(8,128)(2,1)S(1)}, u32[]{:S(2)}, u32[]{:S(2)}) collective-permute-start(bf16[8,2048]{1,0:T(8,128)(2,1)S(1)} %encode.1.own_ref), channel_id=1, source_target_pairs={{0,16},{1,17},{2,18},{3,19},{4,20},{5,21},{6,22},{7,23},{8,24},{9,... | collective-permute-start | bytes 98312 | tf_op jit(solution)/shard_map/ppermute | solution.py:154
  22.2 11.0 %copy-start.5 = (f32[1,2304]{1,0:T(1,128)S(1)}, f32[1,2304]{1,0:T(1,128)}, u32[]{:S(2)}) copy-start(f32[1,2304]{1,0:T(1,128)} %bias_ref.3) | copy-start | bytes 27652

commit v7 on v6

--- a/solution.py
+++ b/solution.py
@@ -32,13 +32,17 @@
 
 
 def prepare_kernel(own_ref, copies_ref):
+    _, parts, columns = copies_ref.shape
     own = own_ref[0].astype(jnp.float32)
+    rows = [own[:, part * columns : (part + 1) * columns] for part in range(parts)]
+    own = jnp.concatenate(rows, axis=0).astype(copies_ref.dtype)
     for copy in range(copies_ref.shape[0]):
         copies_ref[copy] = own
 
 
 def encode_kernel(all_ref, mantissa_ref, exponent_ref, bias_ref, latent_ref):
-    x = all_ref[:, 0, :]
+    parts = all_ref[...].astype(jnp.float32)
+    x = jnp.concatenate([parts[:, part, :] for part in range(parts.shape[1])], axis=1)
     tokens, width = x.shape
     blocks, rows = exponent_ref.shape
     scale = jnp.exp2(exponent_ref[...].astype(jnp.float32)).astype(jnp.bfloat16)
@@ -84,7 +88,11 @@
             body(layer)
 
 
-def decode_chip_kernel(own_ref, core_ref, weight_ref, total_ref):
+def clear_kernel(latent_ref, weight_ref, total_ref):
+    total_ref[...] = jnp.zeros_like(total_ref)
+
+
+def decode_chip_kernel(zero_ref, own_ref, core_ref, weight_ref, total_ref):
     layers = total_ref.shape[0]
 
     def body(layer):
@@ -94,7 +102,7 @@
             if reached:
                 total_ref[target] = products(reached, weight_ref, target)
             else:
-                total_ref[target] = jnp.zeros(total_ref.shape[1:], total_ref.dtype)
+                total_ref[target] = zero_ref[target]
 
     on_each_layer(layers, body)
 
@@ -157,18 +165,22 @@
             [(place(l, f), place(l ^ layer_bit, f ^ feat_bit)) for l, f in everywhere if l % 2 in parities],
         )
 
-    copies = kernel(prepare_kernel, jax.ShapeDtypeStruct((tokens, 1, width), jnp.float32), "prepare", work=20 * WORK)(resid_stream)
+    halves = 2 if width % (2 * BLK) == 0 else 1
+    copies = kernel(
+        prepare_kernel, jax.ShapeDtypeStruct((tokens, halves, width // halves), resid_stream.dtype), "prepare", work=20 * WORK
+    )(resid_stream)
     gathered = lax.all_to_all(copies, "feat", 0, 0, tiled=True)
     latent = kernel(encode_kernel, jax.ShapeDtypeStruct((tokens, feat_local), jnp.bfloat16), "encode")(
         gathered, enc_mantissa[0], jnp.swapaxes(enc_exponent[0], 0, 1), enc_bias
     )
     weight = jnp.swapaxes(dec_weight, 1, 2)
     total = jax.ShapeDtypeStruct((layer_count, tokens, col_local), jnp.float32)
-    core = swap(latent, layer_bit=1)
     other = swap(latent, layer_bit=3)
-    held, core = lax.optimization_barrier((latent, core))
+    zero = kernel(clear_kernel, total, "clear")(latent, weight)
+    held, zero = lax.optimization_barrier((latent, zero))
+    core = swap(held, layer_bit=1)
     same = swap(held, layer_bit=2)
-    chip_total = kernel(decode_chip_kernel, total, "decode_chip")(latent, core, weight)
+    chip_total = kernel(decode_chip_kernel, total, "decode_chip")(zero, latent, core, weight)
     most_total = kernel(functools.partial(decode_more_kernel, 3), total, "decode_other")(chip_total, other, weight)
     parts = kernel(
         decode_last_kernel, jax.ShapeDtypeStruct((layer_count * tokens, 1, col_local), jnp.float32), "decode_same"

time: 34.2 us -> 33.7 us (0.985)
  starting transfers between devices: 2.78 us -> 2.21 us
    ppermute x3, starting transfers between devices: 2.78 us -> 2.21 us  [swap(): lax.ppermute(array, AXES, [(place(l, f), place(l ^ layer_bit, f ^ feat_bi...]
    all_to_all x1, blocking collectives: 9.12 us -> 9.48 us  [shards(): arrived = lax.all_to_all(parts, AXES, 0, 0, tiled=True)]
    pallas_call x6 -> x7, Pallas kernels: 6.81 us -> 6.83 us  [call(): pl.pallas_call(body, out_shape=out_shape, in_specs=[VMEM] * len(operands)...]
where the time goes in v7:
time: 33.7 us; the launch traced here: 33.5 us
  blocking collectives  23.5 us (70%)
  Pallas kernels  6.83 us (20%)
  starting transfers between devices  2.21 us (7%)
  local copies, waits for them, and re-layouts  0.88 us (3%)
    all_to_all x1, blocking collectives, shards(): gathered = lax.all_to_all(copies, 'feat', 0, 0, tiled=True)  14 us
    all_to_all x1, blocking collectives, shards(): arrived = lax.all_to_all(parts, AXES, 0, 0, tiled=True)  9.48 us
    pallas_call x7, Pallas kernels, call(): pl.pallas_call(body, out_shape=out_shape, in_specs=[VMEM] * len(operands)...  6.83 us
    ppermute x3, starting transfers between devices, swap(): lax.ppermute(array, AXES, [(place(l, f), place(l ^ layer_bit, f ^ feat_bi...  2.21 us
    unnamed x12, local copies, waits for them, and re-layouts  0.88 us
  transfers between devices with their start and end apart: 3, of which 0 were waited for; matrix products, arithmetic and copies ran while one was open for 0% of the time, Pallas kernels for 10%

profile of v7, /device:TPU:0, one launch (start us, length us, event | category | flops | bytes accessed | tf_op | source)
XLA Modules:
  0.0 33.5 jit_solution(2710681064152380930)
XLA Ops:
  0.0 0.0 copy-start.1
  0.0 0.0 copy-start.2
  0.0 0.0 copy-start.3
  0.0 0.0 copy-start.4
  0.0 0.8 %copy-done.4 = bf16[1,1,2304]{2,1,0:T(2,128)(2,1)S(1)} copy-done((bf16[1,1,2304]{2,1,0:T(2,128)(2,1)S(1)}, bf16[1,1,2304]{2,1,0:T(2,128)(2,1)}, u32[]{:S(2)}) %copy-start.4) | copy-done | bytes 4632
  0.9 0.0 copy-start
  0.9 14.0 %all_to_all.10.all_ref = bf16[8,2,1152]{2,1,0:T(2,128)(2,1)S(1)} all-to-all(bf16[8,2,1152]{2,1,0:T(2,128)(2,1)S(1)} %prepare.1), channel_id=1, replica_groups=mesh['layer'=4,'feat'=8] {'feat'}, dimensions={0} | all-to-all | bytes 73728 | tf_op jit(solution)/shard_map/all_to_all | solution.py:172
  14.9 0.0 copy-done.1
  14.9 0.0 copy-done.2
  14.9 0.0 copy-done.3
  14.9 1.4 %encode.1.latent_ref.own_ref = bf16[8,2048]{1,0:T(8,128)(2,1)S(1)} custom-call(bf16[8,2,1152]{2,1,0:T(2,128)(2,1)S(1)} %all_to_all.10.all_ref, bf16[2304,2048]{1,0:T(8,128)(2,1)S(1)} %bitcast.10, s32[16,18]{1,0:T(8,128)S(1)} %bitcast.12, f32[1,2048]{1,0:T(1,128)S(1)} %copy-done.3), custom_call_target="tpu_custom_call" | custom-call | flops 2000000000 | tf_op jit(solution)/shard_map/encode/pallas_call | solution.py:20
  16.4 0.0 copy-done
  16.4 0.1 collective-permute-start
  16.5 1.6 %collective-permute-start.1 = (bf16[8,2048]{1,0:T(8,128)(2,1)S(1)}, bf16[8,2048]{1,0:T(8,128)(2,1)S(1)}, u32[]{:S(2)}, u32[]{:S(2)}) collective-permute-start(bf16[8,2048]{1,0:T(8,128)(2,1)S(1)} %encode.1.latent_ref.own_ref), channel_id=1, source_target_pairs={{0,24},{1,25},{2,26},{3,27},{4,28},{5,29},{6,30},{7,31},{8,16},{9,... | collective-permute-start | bytes 98312 | tf_op jit(solution)/shard_map/ppermute | solution.py:162
  18.1 0.5 %collective-permute-start.2 = (bf16[8,2048]{1,0:T(8,128)(2,1)S(1)}, bf16[8,2048]{1,0:T(8,128)(2,1)S(1)}, u32[]{:S(2)}, u32[]{:S(2)}) collective-permute-start(bf16[8,2048]{1,0:T(8,128)(2,1)S(1)} %encode.1.latent_ref.own_ref), channel_id=1, source_target_pairs={{0,16},{1,17},{2,18},{3,19},{4,20},{5,21},{6,22},{7,23},{8,24},{9,... | collective-permute-start | bytes 98312 | tf_op jit(solution)/shard_map/ppermute | solution.py:162
  18.6 0.0 collective-permute-done.core_ref
  18.6 2.8 %decode_chip.1.total_ref = f32[4,8,576]{2,1,0:T(8,128)S(1)} custom-call(f32[4,8,576]{2,1,0:T(8,128)S(1)} %clear.1.zero_ref, bf16[8,2048]{1,0:T(8,128)(2,1)S(1)} %encode.1.latent_ref.own_ref, bf16[8,2048]{1,0:T(8,128)(2,1)S(1)} %collective-permute-done.core_ref, bf16[10,576,2048]{2,1,0:T(8,128)(2,1)S(1)} %bitcast.7), custom_call_target="tpu_custom_call" | custom-call | flops 2000000000 | tf_op jit(solution)/shard_map/decode_chip/pallas_call | solution.py:20
  21.4 0.0 copy-start.5
  21.4 0.0 collective-permute-done.1.latent_ref
  21.4 0.7 %decode_other.1.total_ref = f32[4,8,576]{2,1,0:T(8,128)S(1)} custom-call(f32[4,8,576]{2,1,0:T(8,128)S(1)} %decode_chip.1.total_ref, bf16[8,2048]{1,0:T(8,128)(2,1)S(1)} %collective-permute-done.1.latent_ref, bf16[10,576,2048]{2,1,0:T(8,128)(2,1)S(1)} %bitcast.8), custom_call_target="tpu_custom_call" | custom-call | flops 2000000000 | tf_op jit(solution)/shard_map/decode_other/pallas_call | solution.py:20
  22.1 0.0 collective-permute-done.2.last_ref
  22.1 1.1 %decode_same.1 = f32[32,1,576]{2,1,0:T(1,128)S(1)} custom-call(f32[4,8,576]{2,1,0:T(8,128)S(1)} %decode_other.1.total_ref, bf16[8,2048]{1,0:T(8,128)(2,1)S(1)} %collective-permute-done.2.last_ref, bf16[10,576,2048]{2,1,0:T(8,128)(2,1)S(1)} %bitcast.9), custom_call_target="tpu_custom_call" | custom-call | flops 2000000000 | tf_op jit(solution)/shard_map/decode_same/pallas_call | solution.py:20
  23.2 9.5 %all_to_all.11 = f32[32,1,576]{2,1,0:T(1,128)S(1)} all-to-all(f32[32,1,576]{2,1,0:T(1,128)S(1)} %decode_same.1), channel_id=1, replica_groups=mesh['layer'=4,'feat'=8] {'layer','feat'}, dimensions={0} | all-to-all | bytes 147456 | tf_op jit(solution)/shard_map/all_to_all | solution.py:188
  32.7 0.0 copy-done.5
  32.7 0.7 %finish.1 = bf16[1,1,2304]{2,1,0:T(2,128)(2,1)} custom-call(f32[4,8,1,576]{3,2,1,0:T(1,128)S(1)} %bitcast.11, f32[1,2304]{1,0:T(1,128)S(1)} %copy-done.5), custom_call_target="tpu_custom_call" | custom-call | flops 2000000000 | tf_op jit(solution)/shard_map/finish/pallas_call | solution.py:20
  (2 shorter events, 0.0 us)
Async XLA Ops:
  0.0 14.9 %copy-start.1 = (bf16[1,2304,2048]{2,1,0:T(8,128)(2,1)S(1)}, bf16[1,2304,2048]{2,1,0:T(8,128)(2,1)}, u32[]{:S(2)}) copy-start(bf16[1,2304,2048]{2,1,0:T(8,128)(2,1)} %param.7) | copy-start | bytes 28311556
  0.0 14.9 %copy-start.2 = (s32[1,18,16]{1,2,0:T(8,128)S(1)}, s32[1,18,16]{1,2,0:T(8,128)}, u32[]{:S(2)}) copy-start(s32[1,18,16]{1,2,0:T(8,128)} %param.8) | copy-start | bytes 3460
  0.0 14.9 %copy-start.3 = (f32[1,2048]{1,0:T(1,128)S(1)}, f32[1,2048]{1,0:T(1,128)}, u32[]{:S(2)}) copy-start(f32[1,2048]{1,0:T(1,128)} %bias_ref.2) | copy-start | bytes 24580
  0.0 0.8 %copy-start.4 = (bf16[1,1,2304]{2,1,0:T(2,128)(2,1)S(1)}, bf16[1,1,2304]{2,1,0:T(2,128)(2,1)}, u32[]{:S(2)}) copy-start(bf16[1,1,2304]{2,1,0:T(2,128)(2,1)} %own_ref.1) | copy-start | bytes 13828
  0.9 15.5 %copy-start = (bf16[10,2048,576]{1,2,0:T(8,128)(2,1)S(1)}, bf16[10,2048,576]{1,2,0:T(8,128)(2,1)}, u32[]{:S(2)}) copy-start(bf16[10,2048,576]{1,2,0:T(8,128)(2,1)} %param.10) | copy-start | bytes 70778880
  16.4 2.2 %collective-permute-start = (bf16[8,2048]{1,0:T(8,128)(2,1)S(1)}, bf16[8,2048]{1,0:T(8,128)(2,1)S(1)}, u32[]{:S(2)}, u32[]{:S(2)}) collective-permute-start(bf16[8,2048]{1,0:T(8,128)(2,1)S(1)} %encode.1.latent_ref.own_ref), channel_id=1, source_target_pairs={{0,8},{1,9},{2,10},{3,11},{4,12},{5,13},{6,14},{7,15},{8,0},{9,1},... | collective-permute-start | bytes 98312 | tf_op jit(solution)/shard_map/ppermute | solution.py:162
  16.5 4.9 %collective-permute-start.1 = (bf16[8,2048]{1,0:T(8,128)(2,1)S(1)}, bf16[8,2048]{1,0:T(8,128)(2,1)S(1)}, u32[]{:S(2)}, u32[]{:S(2)}) collective-permute-start(bf16[8,2048]{1,0:T(8,128)(2,1)S(1)} %encode.1.latent_ref.own_ref), channel_id=1, source_target_pairs={{0,24},{1,25},{2,26},{3,27},{4,28},{5,29},{6,30},{7,31},{8,16},{9,... | collective-permute-start | bytes 98312 | tf_op jit(solution)/shard_map/ppermute | solution.py:162
  18.1 4.0 %collective-permute-start.2 = (bf16[8,2048]{1,0:T(8,128)(2,1)S(1)}, bf16[8,2048]{1,0:T(8,128)(2,1)S(1)}, u32[]{:S(2)}, u32[]{:S(2)}) collective-permute-start(bf16[8,2048]{1,0:T(8,128)(2,1)S(1)} %encode.1.latent_ref.own_ref), channel_id=1, source_target_pairs={{0,16},{1,17},{2,18},{3,19},{4,20},{5,21},{6,22},{7,23},{8,24},{9,... | collective-permute-start | bytes 98312 | tf_op jit(solution)/shard_map/ppermute | solution.py:162
  21.4 11.3 %copy-start.5 = (f32[1,2304]{1,0:T(1,128)S(1)}, f32[1,2304]{1,0:T(1,128)}, u32[]{:S(2)}) copy-start(f32[1,2304]{1,0:T(1,128)} %bias_ref.3) | copy-start | bytes 27652

commit v8 on v7

--- a/solution.py
+++ b/solution.py
@@ -130,20 +130,26 @@
             total = total_ref[target]
             if source <= target:
                 total = total + products([(source, last_ref[...])], weight_ref, target)
+            piece = out_ref.shape[2]
+            rest = 2 * piece - total.shape[1]
+            first = total[:, :piece]
+            second = jnp.concatenate([total[:, piece:], jnp.zeros((tokens, rest), total.dtype)], axis=1)
             for token in range(tokens):
-                out_ref[target * tokens + token] = total[token : token + 1, :]
+                rows = jnp.concatenate([first[token : token + 1, :], second[token : token + 1, :]], axis=0)
+                out_ref[target * tokens + token] = rows.astype(out_ref.dtype)
 
     on_each_layer(layers, body)
 
 
-def finish_kernel(parts_ref, bias_ref, out_ref):
-    layers, shards, columns = parts_ref.shape[0], parts_ref.shape[1], parts_ref.shape[3]
+def finish_kernel(columns, parts_ref, bias_ref, out_ref):
+    layers, shards, _, piece = parts_ref.shape
     for block in range(layers):
-        there = slice(block * columns, (block + 1) * columns)
-        total = parts_ref[block, 0]
+        total = parts_ref[block, 0].astype(jnp.float32)
         for shard in range(1, shards):
-            total = total + parts_ref[block, shard]
-        out_ref[:, 0, there] = (total + bias_ref[:, there]).astype(out_ref.dtype)
+            total = total + parts_ref[block, shard].astype(jnp.float32)
+        for row, start, stop in ((0, 0, piece), (1, piece, columns)):
+            there = slice(block * columns + start, block * columns + stop)
+            out_ref[:, 0, there] = (total[row : row + 1, : stop - start] + bias_ref[:, there]).astype(out_ref.dtype)
 
 
 def shards(resid_stream, enc_mantissa, enc_exponent, enc_bias, dec_weight, dec_bias):
@@ -166,6 +172,7 @@
         )
 
     halves = 2 if width % (2 * BLK) == 0 else 1
+    piece = -(-col_local // (2 * BLK)) * BLK
     copies = kernel(
         prepare_kernel, jax.ShapeDtypeStruct((tokens, halves, width // halves), resid_stream.dtype), "prepare", work=20 * WORK
     )(resid_stream)
@@ -183,11 +190,11 @@
     chip_total = kernel(decode_chip_kernel, total, "decode_chip")(zero, latent, core, weight)
     most_total = kernel(functools.partial(decode_more_kernel, 3), total, "decode_other")(chip_total, other, weight)
     parts = kernel(
-        decode_last_kernel, jax.ShapeDtypeStruct((layer_count * tokens, 1, col_local), jnp.float32), "decode_same"
+        decode_last_kernel, jax.ShapeDtypeStruct((layer_count * tokens, 2, piece), jnp.bfloat16), "decode_same"
     )(most_total, same, weight)
     arrived = lax.all_to_all(parts, AXES, 0, 0, tiled=True)
-    return kernel(finish_kernel, jax.ShapeDtypeStruct((tok_local, 1, width), jnp.bfloat16), "finish")(
-        arrived.reshape(layer_count, feat_count, tok_local, col_local), dec_bias
+    return kernel(functools.partial(finish_kernel, col_local), jax.ShapeDtypeStruct((tok_local, 1, width), jnp.bfloat16), "finish")(
+        arrived.reshape(layer_count, feat_count, 2, piece), dec_bias
     )
 
 

time: 33.7 us -> 33.6 us (level)
  no operation moved by 1% of the time
where the time goes in v8:
time: 33.6 us; the launch traced here: 33.3 us
  blocking collectives  23.3 us (69%)
  Pallas kernels  6.85 us (20%)
  starting transfers between devices  2.21 us (7%)
  local copies, waits for them, and re-layouts  0.88 us (3%)
    all_to_all x1, blocking collectives, shards(): gathered = lax.all_to_all(copies, 'feat', 0, 0, tiled=True)  14 us
    all_to_all x1, blocking collectives, shards(): arrived = lax.all_to_all(parts, AXES, 0, 0, tiled=True)  9.27 us
    pallas_call x7, Pallas kernels, call(): pl.pallas_call(body, out_shape=out_shape, in_specs=[VMEM] * len(operands)...  6.85 us
    ppermute x3, starting transfers between devices, swap(): lax.ppermute(array, AXES, [(place(l, f), place(l ^ layer_bit, f ^ feat_bi...  2.21 us
    unnamed x12, local copies, waits for them, and re-layouts  0.88 us
  transfers between devices with their start and end apart: 3, of which 0 were waited for; matrix products, arithmetic and copies ran while one was open for 0% of the time, Pallas kernels for 10%

profile of v8, /device:TPU:0, one launch (start us, length us, event | category | flops | bytes accessed | tf_op | source)
XLA Modules:
  0.0 33.3 jit_solution(4004305372670151371)
XLA Ops:
  0.0 0.0 copy-start.1
  0.0 0.0 copy-start.2
  0.0 0.0 copy-start.3
  0.0 0.0 copy-start.4
  0.0 0.8 %copy-done.4 = bf16[1,1,2304]{2,1,0:T(2,128)(2,1)S(1)} copy-done((bf16[1,1,2304]{2,1,0:T(2,128)(2,1)S(1)}, bf16[1,1,2304]{2,1,0:T(2,128)(2,1)}, u32[]{:S(2)}) %copy-start.4) | copy-done | bytes 4632
  0.9 0.0 copy-start
  0.9 14.0 %all_to_all.10.all_ref = bf16[8,2,1152]{2,1,0:T(2,128)(2,1)S(1)} all-to-all(bf16[8,2,1152]{2,1,0:T(2,128)(2,1)S(1)} %prepare.1), channel_id=1, replica_groups=mesh['layer'=4,'feat'=8] {'feat'}, dimensions={0} | all-to-all | bytes 73728 | tf_op jit(solution)/shard_map/all_to_all | solution.py:179
  14.9 0.0 copy-done.1
  14.9 0.0 copy-done.2
  14.9 0.0 copy-done.3
  14.9 1.4 %encode.1.latent_ref.own_ref = bf16[8,2048]{1,0:T(8,128)(2,1)S(1)} custom-call(bf16[8,2,1152]{2,1,0:T(2,128)(2,1)S(1)} %all_to_all.10.all_ref, bf16[2304,2048]{1,0:T(8,128)(2,1)S(1)} %bitcast.10, s32[16,18]{1,0:T(8,128)S(1)} %bitcast.12, f32[1,2048]{1,0:T(1,128)S(1)} %copy-done.3), custom_call_target="tpu_custom_call" | custom-call | flops 2000000000 | tf_op jit(solution)/shard_map/encode/pallas_call | solution.py:20
  16.4 0.0 copy-done
  16.4 0.1 collective-permute-start
  16.5 1.6 %collective-permute-start.1 = (bf16[8,2048]{1,0:T(8,128)(2,1)S(1)}, bf16[8,2048]{1,0:T(8,128)(2,1)S(1)}, u32[]{:S(2)}, u32[]{:S(2)}) collective-permute-start(bf16[8,2048]{1,0:T(8,128)(2,1)S(1)} %encode.1.latent_ref.own_ref), channel_id=1, source_target_pairs={{0,24},{1,25},{2,26},{3,27},{4,28},{5,29},{6,30},{7,31},{8,16},{9,... | collective-permute-start | bytes 98312 | tf_op jit(solution)/shard_map/ppermute | solution.py:168
  18.1 0.5 %collective-permute-start.2 = (bf16[8,2048]{1,0:T(8,128)(2,1)S(1)}, bf16[8,2048]{1,0:T(8,128)(2,1)S(1)}, u32[]{:S(2)}, u32[]{:S(2)}) collective-permute-start(bf16[8,2048]{1,0:T(8,128)(2,1)S(1)} %encode.1.latent_ref.own_ref), channel_id=1, source_target_pairs={{0,16},{1,17},{2,18},{3,19},{4,20},{5,21},{6,22},{7,23},{8,24},{9,... | collective-permute-start | bytes 98312 | tf_op jit(solution)/shard_map/ppermute | solution.py:168
  18.6 0.0 collective-permute-done.core_ref
  18.6 2.8 %decode_chip.1.total_ref = f32[4,8,576]{2,1,0:T(8,128)S(1)} custom-call(f32[4,8,576]{2,1,0:T(8,128)S(1)} %clear.1.zero_ref, bf16[8,2048]{1,0:T(8,128)(2,1)S(1)} %encode.1.latent_ref.own_ref, bf16[8,2048]{1,0:T(8,128)(2,1)S(1)} %collective-permute-done.core_ref, bf16[10,576,2048]{2,1,0:T(8,128)(2,1)S(1)} %bitcast.7), custom_call_target="tpu_custom_call" | custom-call | flops 2000000000 | tf_op jit(solution)/shard_map/decode_chip/pallas_call | solution.py:20
  21.4 0.0 copy-start.5
  21.4 0.0 collective-permute-done.1.latent_ref
  21.4 0.7 %decode_other.1.total_ref = f32[4,8,576]{2,1,0:T(8,128)S(1)} custom-call(f32[4,8,576]{2,1,0:T(8,128)S(1)} %decode_chip.1.total_ref, bf16[8,2048]{1,0:T(8,128)(2,1)S(1)} %collective-permute-done.1.latent_ref, bf16[10,576,2048]{2,1,0:T(8,128)(2,1)S(1)} %bitcast.8), custom_call_target="tpu_custom_call" | custom-call | flops 2000000000 | tf_op jit(solution)/shard_map/decode_other/pallas_call | solution.py:20
  22.1 0.0 collective-permute-done.2.last_ref
  22.1 1.2 %decode_same.1 = bf16[32,2,384]{2,1,0:T(2,128)(2,1)S(1)} custom-call(f32[4,8,576]{2,1,0:T(8,128)S(1)} %decode_other.1.total_ref, bf16[8,2048]{1,0:T(8,128)(2,1)S(1)} %collective-permute-done.2.last_ref, bf16[10,576,2048]{2,1,0:T(8,128)(2,1)S(1)} %bitcast.9), custom_call_target="tpu_custom_call" | custom-call | flops 2000000000 | tf_op jit(solution)/shard_map/decode_same/pallas_call | solution.py:20
  23.3 9.3 %all_to_all.11 = bf16[32,2,384]{2,1,0:T(2,128)(2,1)S(1)} all-to-all(bf16[32,2,384]{2,1,0:T(2,128)(2,1)S(1)} %decode_same.1), channel_id=1, replica_groups=mesh['layer'=4,'feat'=8] {'layer','feat'}, dimensions={0} | all-to-all | bytes 98304 | tf_op jit(solution)/shard_map/all_to_all | solution.py:195
  32.5 0.0 copy-done.5
  32.5 0.8 %finish.1 = bf16[1,1,2304]{2,1,0:T(2,128)(2,1)} custom-call(bf16[4,8,2,384]{3,2,1,0:T(2,128)(2,1)S(1)} %bitcast.11, f32[1,2304]{1,0:T(1,128)S(1)} %copy-done.5), custom_call_target="tpu_custom_call" | custom-call | flops 2000000000 | tf_op jit(solution)/shard_map/finish/pallas_call | solution.py:20
  (2 shorter events, 0.0 us)
Async XLA Ops:
  0.0 14.9 %copy-start.1 = (bf16[1,2304,2048]{2,1,0:T(8,128)(2,1)S(1)}, bf16[1,2304,2048]{2,1,0:T(8,128)(2,1)}, u32[]{:S(2)}) copy-start(bf16[1,2304,2048]{2,1,0:T(8,128)(2,1)} %param.7) | copy-start | bytes 28311556
  0.0 14.9 %copy-start.2 = (s32[1,18,16]{1,2,0:T(8,128)S(1)}, s32[1,18,16]{1,2,0:T(8,128)}, u32[]{:S(2)}) copy-start(s32[1,18,16]{1,2,0:T(8,128)} %param.8) | copy-start | bytes 3460
  0.0 14.9 %copy-start.3 = (f32[1,2048]{1,0:T(1,128)S(1)}, f32[1,2048]{1,0:T(1,128)}, u32[]{:S(2)}) copy-start(f32[1,2048]{1,0:T(1,128)} %bias_ref.2) | copy-start | bytes 24580
  0.0 0.8 %copy-start.4 = (bf16[1,1,2304]{2,1,0:T(2,128)(2,1)S(1)}, bf16[1,1,2304]{2,1,0:T(2,128)(2,1)}, u32[]{:S(2)}) copy-start(bf16[1,1,2304]{2,1,0:T(2,128)(2,1)} %own_ref.1) | copy-start | bytes 13828
  0.9 15.5 %copy-start = (bf16[10,2048,576]{1,2,0:T(8,128)(2,1)S(1)}, bf16[10,2048,576]{1,2,0:T(8,128)(2,1)}, u32[]{:S(2)}) copy-start(bf16[10,2048,576]{1,2,0:T(8,128)(2,1)} %param.10) | copy-start | bytes 70778880
  16.4 2.2 %collective-permute-start = (bf16[8,2048]{1,0:T(8,128)(2,1)S(1)}, bf16[8,2048]{1,0:T(8,128)(2,1)S(1)}, u32[]{:S(2)}, u32[]{:S(2)}) collective-permute-start(bf16[8,2048]{1,0:T(8,128)(2,1)S(1)} %encode.1.latent_ref.own_ref), channel_id=1, source_target_pairs={{0,8},{1,9},{2,10},{3,11},{4,12},{5,13},{6,14},{7,15},{8,0},{9,1},... | collective-permute-start | bytes 98312 | tf_op jit(solution)/shard_map/ppermute | solution.py:168
  16.5 4.9 %collective-permute-start.1 = (bf16[8,2048]{1,0:T(8,128)(2,1)S(1)}, bf16[8,2048]{1,0:T(8,128)(2,1)S(1)}, u32[]{:S(2)}, u32[]{:S(2)}) collective-permute-start(bf16[8,2048]{1,0:T(8,128)(2,1)S(1)} %encode.1.latent_ref.own_ref), channel_id=1, source_target_pairs={{0,24},{1,25},{2,26},{3,27},{4,28},{5,29},{6,30},{7,31},{8,16},{9,... | collective-permute-start | bytes 98312 | tf_op jit(solution)/shard_map/ppermute | solution.py:168
  18.1 4.0 %collective-permute-start.2 = (bf16[8,2048]{1,0:T(8,128)(2,1)S(1)}, bf16[8,2048]{1,0:T(8,128)(2,1)S(1)}, u32[]{:S(2)}, u32[]{:S(2)}) collective-permute-start(bf16[8,2048]{1,0:T(8,128)(2,1)S(1)} %encode.1.latent_ref.own_ref), channel_id=1, source_target_pairs={{0,16},{1,17},{2,18},{3,19},{4,20},{5,21},{6,22},{7,23},{8,24},{9,... | collective-permute-start | bytes 98312 | tf_op jit(solution)/shard_map/ppermute | solution.py:168
  21.4 11.1 %copy-start.5 = (f32[1,2304]{1,0:T(1,128)S(1)}, f32[1,2304]{1,0:T(1,128)}, u32[]{:S(2)}) copy-start(f32[1,2304]{1,0:T(1,128)} %bias_ref.3) | copy-start | bytes 27652

commit v9 on v7

--- a/solution.py
+++ b/solution.py
@@ -29,6 +29,10 @@
         )(*operands)
 
     return call
+
+
+def take_kernel(own_ref, out_ref):
+    out_ref[...] = own_ref[...]
 
 
 def prepare_kernel(own_ref, copies_ref):
@@ -165,10 +169,11 @@
             [(place(l, f), place(l ^ layer_bit, f ^ feat_bit)) for l, f in everywhere if l % 2 in parities],
         )
 
+    own = kernel(take_kernel, jax.ShapeDtypeStruct(resid_stream.shape, resid_stream.dtype), "take", work=1000)(resid_stream)
     halves = 2 if width % (2 * BLK) == 0 else 1
     copies = kernel(
-        prepare_kernel, jax.ShapeDtypeStruct((tokens, halves, width // halves), resid_stream.dtype), "prepare", work=20 * WORK
-    )(resid_stream)
+        prepare_kernel, jax.ShapeDtypeStruct((tokens, halves, width // halves), resid_stream.dtype), "prepare", work=7 * WORK
+    )(own)
     gathered = lax.all_to_all(copies, "feat", 0, 0, tiled=True)
     latent = kernel(encode_kernel, jax.ShapeDtypeStruct((tokens, feat_local), jnp.bfloat16), "encode")(
         gathered, enc_mantissa[0], jnp.swapaxes(enc_exponent[0], 0, 1), enc_bias

time: 33.7 us -> 33.8 us (level)
    unnamed x12 -> x22, local copies, waits for them, and re-layouts: 0.88 us -> 0.77 us
    pallas_call x7 -> x8, Pallas kernels: 6.83 us -> 6.84 us  [call(): pl.pallas_call(body, out_shape=out_shape, in_specs=[VMEM] * len(operands)...]
where the time goes in v9:
time: 33.8 us; the launch traced here: 33.5 us
  blocking collectives  23.6 us (70%)
  Pallas kernels  6.84 us (20%)
  starting transfers between devices  2.21 us (7%)
  local copies, waits for them, and re-layouts  0.77 us (2%)
    all_to_all x1, blocking collectives, shards(): gathered = lax.all_to_all(copies, 'feat', 0, 0, tiled=True)  14 us
    all_to_all x1, blocking collectives, shards(): arrived = lax.all_to_all(parts, AXES, 0, 0, tiled=True)  9.53 us
    pallas_call x8, Pallas kernels, call(): pl.pallas_call(body, out_shape=out_shape, in_specs=[VMEM] * len(operands)...  6.84 us
    ppermute x3, starting transfers between devices, swap(): lax.ppermute(array, AXES, [(place(l, f), place(l ^ layer_bit, f ^ feat_bi...  2.21 us
    unnamed x22, local copies, waits for them, and re-layouts  0.77 us
  transfers between devices with their start and end apart: 3, of which 0 were waited for; matrix products, arithmetic and copies ran while one was open for 0% of the time, Pallas kernels for 10%

profile of v9, /device:TPU:0, one launch (start us, length us, event | category | flops | bytes accessed | tf_op | source)
XLA Modules:
  0.0 33.5 jit_solution(8436732087296862466)
XLA Ops:
  0.0 0.0 copy-start.1
  0.0 0.7 %copy-done.1 = bf16[1,1,2304]{2,1,0:T(2,128)(2,1)S(1)} copy-done((bf16[1,1,2304]{2,1,0:T(2,128)(2,1)S(1)}, bf16[1,1,2304]{2,1,0:T(2,128)(2,1)}, u32[]{:S(2)}) %copy-start.1) | copy-done | bytes 4632
  0.7 0.0 slice-start
  0.7 0.0 copy-start
  0.7 0.0 copy-start.2
  0.7 0.0 copy-start.3
  0.8 0.0 slice-start.1
  0.8 0.0 slice-start.2
  0.8 0.0 slice-start.3
  0.8 0.0 slice-start.4
  0.8 0.0 slice-start.5
  0.8 14.0 %all_to_all.10.all_ref = bf16[8,2,1152]{2,1,0:T(2,128)(2,1)S(1)} all-to-all(bf16[8,2,1152]{2,1,0:T(2,128)(2,1)S(1)} %prepare.1), channel_id=1, replica_groups=mesh['layer'=4,'feat'=8] {'feat'}, dimensions={0} | all-to-all | bytes 73728 | tf_op jit(solution)/shard_map/all_to_all | solution.py:177
  14.9 0.0 copy-done
  14.9 0.0 copy-done.2
  14.9 0.0 copy-done.3
  14.9 1.4 %encode.1.latent_ref.own_ref = bf16[8,2048]{1,0:T(8,128)(2,1)S(1)} custom-call(bf16[8,2,1152]{2,1,0:T(2,128)(2,1)S(1)} %all_to_all.10.all_ref, bf16[2304,2048]{1,0:T(8,128)(2,1)S(1)} %bitcast.12, s32[16,18]{1,0:T(8,128)S(1)} %bitcast.14, f32[1,2048]{1,0:T(1,128)S(1)} %copy-done.3), custom_call_target="tpu_custom_call" | custom-call | flops 2000000000 | tf_op jit(solution)/shard_map/encode/pallas_call | solution.py:20
  16.3 0.0 slice-done
  16.3 0.0 slice-done.1
  16.3 0.0 slice-done.2
  16.4 0.0 slice-done.3
  16.4 0.0 slice-done.4
  16.4 0.0 slice-done.5
  16.4 0.1 collective-permute-start
  16.5 1.6 %collective-permute-start.1 = (bf16[8,2048]{1,0:T(8,128)(2,1)S(1)}, bf16[8,2048]{1,0:T(8,128)(2,1)S(1)}, u32[]{:S(2)}, u32[]{:S(2)}) collective-permute-start(bf16[8,2048]{1,0:T(8,128)(2,1)S(1)} %encode.1.latent_ref.own_ref), channel_id=1, source_target_pairs={{0,24},{1,25},{2,26},{3,27},{4,28},{5,29},{6,30},{7,31},{8,16},{9,... | collective-permute-start | bytes 98312 | tf_op jit(solution)/shard_map/ppermute | solution.py:166
  18.1 0.5 %collective-permute-start.2 = (bf16[8,2048]{1,0:T(8,128)(2,1)S(1)}, bf16[8,2048]{1,0:T(8,128)(2,1)S(1)}, u32[]{:S(2)}, u32[]{:S(2)}) collective-permute-start(bf16[8,2048]{1,0:T(8,128)(2,1)S(1)} %encode.1.latent_ref.own_ref), channel_id=1, source_target_pairs={{0,16},{1,17},{2,18},{3,19},{4,20},{5,21},{6,22},{7,23},{8,24},{9,... | collective-permute-start | bytes 98312 | tf_op jit(solution)/shard_map/ppermute | solution.py:166
  18.6 0.0 collective-permute-done.core_ref
  18.6 2.8 %decode_chip.1.total_ref = f32[4,8,576]{2,1,0:T(8,128)S(1)} custom-call(f32[4,8,576]{2,1,0:T(8,128)S(1)} %clear.1.zero_ref, bf16[8,2048]{1,0:T(8,128)(2,1)S(1)} %encode.1.latent_ref.own_ref, bf16[8,2048]{1,0:T(8,128)(2,1)S(1)} %collective-permute-done.core_ref, bf16[10,576,2048]{2,1,0:T(8,128)(2,1)S(1)} %bitcast.9), custom_call_target="tpu_custom_call" | custom-call | flops 2000000000 | tf_op jit(solution)/shard_map/decode_chip/pallas_call | solution.py:20
  21.4 0.0 copy-start.4
  21.4 0.0 collective-permute-done.1.latent_ref
  21.4 0.7 %decode_other.1.total_ref = f32[4,8,576]{2,1,0:T(8,128)S(1)} custom-call(f32[4,8,576]{2,1,0:T(8,128)S(1)} %decode_chip.1.total_ref, bf16[8,2048]{1,0:T(8,128)(2,1)S(1)} %collective-permute-done.1.latent_ref, bf16[10,576,2048]{2,1,0:T(8,128)(2,1)S(1)} %bitcast.10), custom_call_target="tpu_custom_call" | custom-call | flops 2000000000 | tf_op jit(solution)/shard_map/decode_other/pallas_call | solution.py:20
  22.1 0.0 collective-permute-done.2.last_ref
  22.1 1.1 %decode_same.1 = f32[32,1,576]{2,1,0:T(1,128)S(1)} custom-call(f32[4,8,576]{2,1,0:T(8,128)S(1)} %decode_other.1.total_ref, bf16[8,2048]{1,0:T(8,128)(2,1)S(1)} %collective-permute-done.2.last_ref, bf16[10,576,2048]{2,1,0:T(8,128)(2,1)S(1)} %bitcast.11), custom_call_target="tpu_custom_call" | custom-call | flops 2000000000 | tf_op jit(solution)/shard_map/decode_same/pallas_call | solution.py:20
  23.3 9.5 %all_to_all.11 = f32[32,1,576]{2,1,0:T(1,128)S(1)} all-to-all(f32[32,1,576]{2,1,0:T(1,128)S(1)} %decode_same.1), channel_id=1, replica_groups=mesh['layer'=4,'feat'=8] {'layer','feat'}, dimensions={0} | all-to-all | bytes 147456 | tf_op jit(solution)/shard_map/all_to_all | solution.py:193
  32.8 0.0 copy-done.4
  32.8 0.7 %finish.1 = bf16[1,1,2304]{2,1,0:T(2,128)(2,1)} custom-call(f32[4,8,1,576]{3,2,1,0:T(1,128)S(1)} %bitcast.13, f32[1,2304]{1,0:T(1,128)S(1)} %copy-done.4), custom_call_target="tpu_custom_call" | custom-call | flops 2000000000 | tf_op jit(solution)/shard_map/finish/pallas_call | solution.py:20
  (4 shorter events, 0.0 us)
Async XLA Ops:
  0.0 0.7 %copy-start.1 = (bf16[1,1,2304]{2,1,0:T(2,128)(2,1)S(1)}, bf16[1,1,2304]{2,1,0:T(2,128)(2,1)}, u32[]{:S(2)}) copy-start(bf16[1,1,2304]{2,1,0:T(2,128)(2,1)} %own_ref.1) | copy-start | bytes 13828
  0.7 15.6 %slice-start = ((s8[23592960]{0:T(1024)(128)(4,1)}), s8[4194304]{0:T(1024)(128)(4,1)S(1)}, s32[]{:S(2)}) async-start(s8[23592960]{0:T(1024)(128)(4,1)} %bitcast.6), calls=%async_computation.2 | async-start | bytes 8388608
  0.7 14.1 %copy-start = (bf16[1,2304,2048]{2,1,0:T(8,128)(2,1)S(1)}, bf16[1,2304,2048]{2,1,0:T(8,128)(2,1)}, u32[]{:S(2)}) copy-start(bf16[1,2304,2048]{2,1,0:T(8,128)(2,1)} %param.7) | copy-start | bytes 28311556
  0.7 14.1 %copy-start.2 = (s32[1,18,16]{1,2,0:T(8,128)S(1)}, s32[1,18,16]{1,2,0:T(8,128)}, u32[]{:S(2)}) copy-start(s32[1,18,16]{1,2,0:T(8,128)} %param.8) | copy-start | bytes 3460
  0.7 14.1 %copy-start.3 = (f32[1,2048]{1,0:T(1,128)S(1)}, f32[1,2048]{1,0:T(1,128)}, u32[]{:S(2)}) copy-start(f32[1,2048]{1,0:T(1,128)} %bias_ref.2) | copy-start | bytes 24580
  0.8 15.6 %slice-start.1 = ((s8[23592960]{0:T(1024)(128)(4,1)}), s8[4194304]{0:T(1024)(128)(4,1)S(1)}, s32[]{:S(2)}) async-start(s8[23592960]{0:T(1024)(128)(4,1)} %bitcast.6), calls=%async_computation.3 | async-start | bytes 8388608
  0.8 15.6 %slice-start.2 = ((s8[23592960]{0:T(1024)(128)(4,1)}), s8[4194304]{0:T(1024)(128)(4,1)S(1)}, s32[]{:S(2)}) async-start(s8[23592960]{0:T(1024)(128)(4,1)} %bitcast.6), calls=%async_computation.4 | async-start | bytes 8388608
  0.8 15.6 %slice-start.3 = ((s8[23592960]{0:T(1024)(128)(4,1)}), s8[4194304]{0:T(1024)(128)(4,1)S(1)}, s32[]{:S(2)}) async-start(s8[23592960]{0:T(1024)(128)(4,1)} %bitcast.6), calls=%async_computation.5 | async-start | bytes 8388608
  0.8 15.6 %slice-start.4 = ((s8[23592960]{0:T(1024)(128)(4,1)}), s8[4194304]{0:T(1024)(128)(4,1)S(1)}, s32[]{:S(2)}) async-start(s8[23592960]{0:T(1024)(128)(4,1)} %bitcast.6), calls=%async_computation.6 | async-start | bytes 8388608
  0.8 15.6 %slice-start.5 = ((s8[23592960]{0:T(1024)(128)(4,1)}), s8[2621440]{0:T(1024)(128)(4,1)S(1)}, s32[]{:S(2)}) async-start(s8[23592960]{0:T(1024)(128)(4,1)} %bitcast.6), calls=%async_computation.7 | async-start | bytes 5242880
  16.4 2.2 %collective-permute-start = (bf16[8,2048]{1,0:T(8,128)(2,1)S(1)}, bf16[8,2048]{1,0:T(8,128)(2,1)S(1)}, u32[]{:S(2)}, u32[]{:S(2)}) collective-permute-start(bf16[8,2048]{1,0:T(8,128)(2,1)S(1)} %encode.1.latent_ref.own_ref), channel_id=1, source_target_pairs={{0,8},{1,9},{2,10},{3,11},{4,12},{5,13},{6,14},{7,15},{8,0},{9,1},... | collective-permute-start | bytes 98312 | tf_op jit(solution)/shard_map/ppermute | solution.py:166
  16.5 4.9 %collective-permute-start.1 = (bf16[8,2048]{1,0:T(8,128)(2,1)S(1)}, bf16[8,2048]{1,0:T(8,128)(2,1)S(1)}, u32[]{:S(2)}, u32[]{:S(2)}) collective-permute-start(bf16[8,2048]{1,0:T(8,128)(2,1)S(1)} %encode.1.latent_ref.own_ref), channel_id=1, source_target_pairs={{0,24},{1,25},{2,26},{3,27},{4,28},{5,29},{6,30},{7,31},{8,16},{9,... | collective-permute-start | bytes 98312 | tf_op jit(solution)/shard_map/ppermute | solution.py:166
  18.1 4.0 %collective-permute-start.2 = (bf16[8,2048]{1,0:T(8,128)(2,1)S(1)}, bf16[8,2048]{1,0:T(8,128)(2,1)S(1)}, u32[]{:S(2)}, u32[]{:S(2)}) collective-permute-start(bf16[8,2048]{1,0:T(8,128)(2,1)S(1)} %encode.1.latent_ref.own_ref), channel_id=1, source_target_pairs={{0,16},{1,17},{2,18},{3,19},{4,20},{5,21},{6,22},{7,23},{8,24},{9,... | collective-permute-start | bytes 98312 | tf_op jit(solution)/shard_map/ppermute | solution.py:166
  21.4 11.4 %copy-start.4 = (f32[1,2304]{1,0:T(1,128)S(1)}, f32[1,2304]{1,0:T(1,128)}, u32[]{:S(2)}) copy-start(f32[1,2304]{1,0:T(1,128)} %bias_ref.3) | copy-start | bytes 27652
